TPU v7x, 32 devices: a whole 2x2x4 slice. The times are simulated.
32 devices in a mesh: row: 4 (over y, x), col: 8 (over z, core).
Axes of the slice: x: 2, y: 2, z: 4, core: 2. Of those that a mesh axis runs over, the one named last changes fastest.
Arguments:
- latents: bfloat16 [128, 128, 512], P('row', 'col'), may hold values from -6 to 6
- cotangent: bfloat16 [128, 128, 512], P('row', 'col'), may hold values from -6 to 6
- w_row: bfloat16 [4, 512, 512], replicated, may hold values from -6.6733202 to 6.6733202, as said below
- w_col: bfloat16 [4, 512, 512], replicated, may hold values from -6.6733202 to 6.6733202, as said below
- keep_heads: int32 [2, 8], replicated, may hold values 0 or 1
Outputs:
- output: bfloat16 [128, 128, 512], P('row', 'col')
- grad_latents: bfloat16 [128, 128, 512], P('row', 'col')
- grad_row: float32 [4, 512, 512], replicated
- grad_col: float32 [4, 512, 512], replicated
Inputs may be any that keep to these rules, and one draw needn't show every extreme that they name: `w_row`: projection weights. `w_col`: projection weights.
All inputs are finite; a program needn't handle non-finite values.
Results may differ from a plain program's by a relative error of at most 0.033.
Values may be sent and summed in bfloat16 or wider, within the bound.
A program may use at most 128 MiB of HBM per device.

v0:
```python
import jax
import jax.numpy as jnp
from jax import lax
from jax.sharding import PartitionSpec as P

HEADS = 8
HEAD = 64


EPSILON = 1e-06


def mat_tn(left, right):
    return lax.dot_general(
        left, right, (((0,), (0,)), ((), ())), preferred_element_type=jnp.float32
    )


def mat_nt(left, right):
    return lax.dot_general(
        left, right, (((1,), (1,)), ((), ())), preferred_element_type=jnp.float32
    )


def head_specs(letters):
    if letters == "nl":
        return ("nlhe", "nmhe")
    return ("lnhe", "mnhe")


def line_forward(inputs, weights, head_gain, letters):
    in_shape = inputs.shape
    model_width = in_shape[2]
    q_spec, k_spec = head_specs(letters)
    values_f = inputs.astype(jnp.float32)
    inv_rms = lax.rsqrt(jnp.mean(values_f * values_f, axis=-1, keepdims=True) + EPSILON)
    normed = (values_f * inv_rms).astype(jnp.bfloat16).reshape(-1, model_width)

    def project(which_proj):
        result = jnp.dot(normed, weights[which_proj], preferred_element_type=jnp.float32)
        return result.astype(jnp.bfloat16).reshape(in_shape[0], in_shape[1], HEADS, HEAD)

    q_proj, k_proj, v_proj = (project(0), project(1), project(2))
    scores = jnp.einsum(
        q_spec + "," + k_spec + "->nhlm", q_proj, k_proj, preferred_element_type=jnp.float32
    ) * HEAD ** (-0.5)
    row_max = jnp.max(scores, axis=-1, keepdims=True)
    exp_scores = jnp.exp(scores - row_max)
    attn_probs = exp_scores / jnp.sum(exp_scores, axis=-1, keepdims=True)
    probs_low = attn_probs.astype(jnp.bfloat16)
    mixed_heads = jnp.einsum(
        "nhlm," + k_spec + "->" + q_spec, probs_low, v_proj, preferred_element_type=jnp.float32
    )
    attended = (mixed_heads * head_gain[:, None]).astype(jnp.bfloat16).reshape(-1, model_width)
    result = values_f + jnp.dot(attended, weights[3], preferred_element_type=jnp.float32).reshape(
        in_shape
    )
    saved_state = (normed, q_proj, k_proj, v_proj, attn_probs, probs_low, attended, inv_rms)
    return (result.astype(jnp.bfloat16), saved_state)


def line_backward(grad_out, inputs, saved_state, weights, head_gain, letters):
    normed, q_proj, k_proj, v_proj, attn_probs, probs_low, attended, inv_rms = saved_state
    in_shape = inputs.shape
    model_width = in_shape[2]
    q_spec, k_spec = head_specs(letters)
    grad_flat = grad_out.reshape(-1, model_width)
    grad_wo = mat_tn(attended, grad_flat)
    grad_att = mat_nt(grad_flat, weights[3]).reshape(in_shape[0], in_shape[1], HEADS, HEAD)
    grad_att = (grad_att * head_gain[:, None]).astype(jnp.bfloat16)
    grad_probs = jnp.einsum(
        q_spec + "," + k_spec + "->nhlm", grad_att, v_proj, preferred_element_type=jnp.float32
    )
    grad_scores = (
        attn_probs
        * (grad_probs - jnp.sum(attn_probs * grad_probs, axis=-1, keepdims=True))
        * HEAD ** (-0.5)
    )
    grad_scores = grad_scores.astype(jnp.bfloat16)
    grad_q = jnp.einsum(
        "nhlm," + k_spec + "->" + q_spec, grad_scores, k_proj, preferred_element_type=jnp.float32
    )
    grad_k = jnp.einsum(
        "nhlm," + q_spec + "->" + k_spec, grad_scores, q_proj, preferred_element_type=jnp.float32
    )
    grad_v = jnp.einsum(
        "nhlm," + q_spec + "->" + k_spec, probs_low, grad_att, preferred_element_type=jnp.float32
    )
    grad_q = grad_q.astype(jnp.bfloat16).reshape(-1, model_width)
    grad_k = grad_k.astype(jnp.bfloat16).reshape(-1, model_width)
    grad_v = grad_v.astype(jnp.bfloat16).reshape(-1, model_width)
    grad_weights = jnp.stack(
        [mat_tn(normed, grad_q), mat_tn(normed, grad_k), mat_tn(normed, grad_v), grad_wo]
    )
    grad_normed = (
        mat_nt(grad_q, weights[0]) + mat_nt(grad_k, weights[1]) + mat_nt(grad_v, weights[2])
    )
    values_f = inputs.astype(jnp.float32).reshape(-1, model_width)
    inv_flat = inv_rms.reshape(-1, 1)
    grad_in = grad_flat.astype(jnp.float32) + inv_flat * grad_normed
    grad_in = grad_in - values_f * inv_flat * inv_flat * inv_flat * jnp.mean(
        grad_normed * values_f, axis=-1, keepdims=True
    )
    return (grad_in.astype(jnp.bfloat16).reshape(in_shape), grad_weights)


def to_rows(values):
    return lax.all_to_all(values, "col", split_axis=0, concat_axis=1, tiled=True)


def from_rows(values):
    return lax.all_to_all(values, "col", split_axis=1, concat_axis=0, tiled=True)


def to_cols(values):
    return lax.all_to_all(values, "row", split_axis=1, concat_axis=0, tiled=True)


def from_cols(values):
    return lax.all_to_all(values, "row", split_axis=0, concat_axis=1, tiled=True)


def body(latents, cotangent, w_row, w_col, keep_heads):
    head_gain = keep_heads.astype(jnp.float32)
    rows_input = to_rows(latents)
    mid_rows, saved_row = line_forward(rows_input, w_row, head_gain[0], "nl")
    mid_cols = to_cols(from_rows(mid_rows))
    grad_cols = to_cols(cotangent)
    out_cols, saved_col = line_forward(mid_cols, w_col, head_gain[1], "ln")
    grad_mid_cols, grad_col = line_backward(
        grad_cols, mid_cols, saved_col, w_col, head_gain[1], "ln"
    )
    output = from_cols(out_cols)
    grad_mid_rows = to_rows(from_cols(grad_mid_cols))
    grad_in_rows, grad_row = line_backward(
        grad_mid_rows, rows_input, saved_row, w_row, head_gain[0], "nl"
    )
    grad_latents = from_rows(grad_in_rows)
    grad_row, grad_col = lax.psum((grad_row, grad_col), ("row", "col"))
    return (output, grad_latents, grad_row, grad_col)


def solution(mesh):
    in_specs = (P("row", "col", None), P("row", "col", None), P(), P(), P())
    out_specs = (P("row", "col", None), P("row", "col", None), P(), P())
    return jax.shard_map(body, mesh=mesh, in_specs=in_specs, out_specs=out_specs, check_vma=False)
```

profile of v0, /device:TPU:0, one launch (start us, length us, event | category | flops | bytes accessed | tf_op | source)
XLA Modules:
  0.0 411.9 jit_solution(17925032482751793158)
XLA Ops:
  7.2 6.3 %all-to-all-start = ((bf16[32,16,512]{2,1,0:T(8,128)(2,1)}), bf16[32,16,512]{2,1,0:T(8,128)(2,1)S(1)}, u32[]{:S(2)}, u32[]{:S(2)}) async-start(bf16[32,16,512]{2,1,0:T(8,128)(2,1)} %param.5), calls=%async_computation | async-start | bytes 1048576 | tf_op jit(solution)/shard_map/all_to_all | solution.py:108
  14.2 14.7 %all-to-all-done = bf16[32,16,512]{2,1,0:T(8,128)(2,1)S(1)} async-done(((bf16[32,16,512]{2,1,0:T(8,128)(2,1)}), bf16[32,16,512]{2,1,0:T(8,128)(2,1)S(1)}, u32[]{:S(2)}, u32[]{:S(2)}) %all-to-all-start) | async-done | bytes 524320 | tf_op jit(solution)/shard_map/all_to_all | solution.py:108
  38.6 3.4 fusion.132
  46.3 3.5 all-to-all-start.1
  50.9 14.2 %all-to-all-done.1 = bf16[4,128,512]{2,0,1:T(4,128)(2,1)S(1)} async-done(((bf16[4,128,512]{2,0,1:T(4,128)(2,1)}), bf16[4,128,512]{2,0,1:T(4,128)(2,1)S(1)}, u32[]{:S(2)}, u32[]{:S(2)}) %all-to-all-start.1) | async-done | bytes 524320 | tf_op jit(solution)/shard_map/all_to_all | solution.py:112
  65.0 3.7 all-to-all-start.4
  70.0 6.6 %all-to-all-done.4 = bf16[32,16,512]{2,0,1:T(8,128)(2,1)S(1)} async-done(((bf16[32,16,512]{2,0,1:T(8,128)(2,1)}), bf16[32,16,512]{2,0,1:T(8,128)(2,1)S(1)}, u32[]{:S(2)}, u32[]{:S(2)}) %all-to-all-start.4) | async-done | bytes 524320 | tf_op jit(solution)/shard_map/all_to_all | solution.py:116
  76.6 3.6 all-to-all-start.2
  107.7 5.0 %fusion.47 = bf16[128,4,8,64]{0,3,2,1:T(8,128)(2,1)} fusion(bf16[128,4,8,64]{0,3,2,1:T(8,128)(2,1)S(1)} %copy-done.31, f32[4,8,128,128]{2,3,1,0:T(8,128)} %fusion.134, f32[4,8,128,128]{2,3,1,0:T(8,128)} %get-tuple-element.11, f32[4,8,128]{2,1,0:T(8,128)S(1)} %get-tuple-element.10), kind=kOutput, calls=%fused_computation.61 | convolution fusion | flops 71045248 | bytes 5259264 | tf_op jit(solution)/shard_map/nhlm,mnhe->lnhe/dot_general | solution.py:80
  112.7 5.1 %fusion.44 = bf16[128,4,8,64]{0,3,2,1:T(8,128)(2,1)} fusion(bf16[128,4,8,64]{0,3,2,1:T(8,128)(2,1)S(1)} %copy-done.32, f32[4,8,128,128]{2,3,1,0:T(8,128)} %fusion.134, f32[4,8,128,128]{2,3,1,0:T(8,128)} %get-tuple-element.11, f32[4,8,128]{2,1,0:T(8,128)S(1)} %get-tuple-element.10), kind=kOutput, calls=%fused_computation.60 | convolution fusion | flops 71045248 | bytes 5259264 | tf_op jit(solution)/shard_map/nhlm,lnhe->mnhe/dot_general | solution.py:83
  124.5 3.3 copy.219
  130.4 3.3 copy.217
  136.5 3.3 copy.214
  150.4 4.1 %all-to-all-start.5 = ((bf16[128,4,512]{2,1,0:T(4,128)(2,1)}), bf16[128,4,512]{2,1,0:T(4,128)(2,1)}, u32[]{:S(2)}, u32[]{:S(2)}) async-start(bf16[128,4,512]{2,1,0:T(4,128)(2,1)} %reshape.260), calls=%async_computation.5 | async-start | bytes 1048576 | tf_op jit(solution)/shard_map/all_to_all | solution.py:120
  163.8 4.1 %all-to-all-start.6 = ((bf16[32,16,512]{2,1,0:T(8,128)(2,1)}), bf16[32,16,512]{2,1,0:T(8,128)(2,1)}, u32[]{:S(2)}, u32[]{:S(2)}) async-start(bf16[32,16,512]{2,1,0:T(8,128)(2,1)} %copy.223), calls=%async_computation.6 | async-start | bytes 1048576 | tf_op jit(solution)/shard_map/all_to_all | solution.py:108
  174.0 9.3 %all-to-all-done.6 = bf16[32,16,512]{2,1,0:T(8,128)(2,1)} async-done(((bf16[32,16,512]{2,1,0:T(8,128)(2,1)}), bf16[32,16,512]{2,1,0:T(8,128)(2,1)}, u32[]{:S(2)}, u32[]{:S(2)}) %all-to-all-start.6) | async-done | bytes 524320 | tf_op jit(solution)/shard_map/all_to_all | solution.py:108
  188.5 5.1 %fusion.53 = bf16[4,128,8,64]{1,3,2,0:T(8,128)(2,1)} fusion(bf16[4,128,8,64]{1,3,2,0:T(8,128)(2,1)S(1)} %copy-done.30, f32[4,8,128,128]{2,3,1,0:T(8,128)} %fusion.135, f32[4,8,128,128]{2,3,1,0:T(8,128)} %get-tuple-element.9, f32[4,8,128]{2,1,0:T(8,128)S(1)} %get-tuple-element.8), kind=kOutput, calls=%fused_computation.63 | convolution fusion | flops 71045248 | bytes 5259264 | tf_op jit(solution)/shard_map/nhlm,nmhe->nlhe/dot_general | solution.py:80
  193.6 5.2 %fusion.50 = bf16[4,128,8,64]{1,3,2,0:T(8,128)(2,1)} fusion(bf16[4,128,8,64]{1,3,2,0:T(8,128)(2,1)} %copy.189, f32[4,8,128,128]{2,3,1,0:T(8,128)} %fusion.135, f32[4,8,128,128]{2,3,1,0:T(8,128)} %get-tuple-element.9, f32[4,8,128]{2,1,0:T(8,128)S(1)} %get-tuple-element.8), kind=kOutput, calls=%fused_computation.62 | convolution fusion | flops 71045248 | bytes 5259264 | tf_op jit(solution)/shard_map/nhlm,nlhe->nmhe/dot_general | solution.py:83
  210.2 4.2 %all-to-all-start.3 = ((bf16[128,4,512]{2,1,0:T(4,128)(2,1)}), bf16[128,4,512]{2,1,0:T(4,128)(2,1)S(1)}, u32[]{:S(2)}, u32[]{:S(2)}) async-start(bf16[128,4,512]{2,1,0:T(4,128)(2,1)} %copy.205), calls=%async_computation.3 | async-start | bytes 1048576 | tf_op jit(solution)/shard_map/all_to_all | solution.py:120
  219.5 9.3 %all-to-all-done.3 = bf16[128,4,512]{2,1,0:T(4,128)(2,1)S(1)} async-done(((bf16[128,4,512]{2,1,0:T(4,128)(2,1)}), bf16[128,4,512]{2,1,0:T(4,128)(2,1)S(1)}, u32[]{:S(2)}, u32[]{:S(2)}) %all-to-all-start.3) | async-done | bytes 524320 | tf_op jit(solution)/shard_map/all_to_all | solution.py:120
  228.8 3.5 all-to-all-start.7
  233.5 19.3 %all-to-all-done.7 = bf16[4,128,512]{2,0,1:T(4,128)(2,1)S(1)} async-done(((bf16[4,128,512]{2,0,1:T(4,128)(2,1)}), bf16[4,128,512]{2,0,1:T(4,128)(2,1)S(1)}, u32[]{:S(2)}, u32[]{:S(2)}) %all-to-all-start.7) | async-done | bytes 524320 | tf_op jit(solution)/shard_map/all_to_all | solution.py:112
  253.8 144.0 %all-reduce.3.cloned.1.call-done = (f32[4,512,512]{2,1,0:T(8,128)}, f32[4,512,512]{2,1,0:T(8,128)}) async-done(((f32[4,512,512]{2,1,0:T(8,128)}, f32[4,512,512]{2,1,0:T(8,128)}), (f32[4,512,512]{2,1,0:T(8,128)}, f32[4,512,512]{2,1,0:T(8,128)})) %all-reduce.3.cloned.1.call-update) | async-done | bytes 8388624 | tf_op jit(solution)/shard_map/psum | solution.py:139
  397.8 4.8 %copy.296 = f32[4,512,512]{2,1,0:T(8,128)} copy(f32[4,512,512]{2,1,0:T(8,128)} %get-tuple-element.18) | data formatting | bytes 8388608
  (182 shorter events, 107.5 us)
Async XLA Ops:
  7.2 21.7 %all-to-all-start = ((bf16[32,16,512]{2,1,0:T(8,128)(2,1)}), bf16[32,16,512]{2,1,0:T(8,128)(2,1)S(1)}, u32[]{:S(2)}, u32[]{:S(2)}) async-start(bf16[32,16,512]{2,1,0:T(8,128)(2,1)} %param.5), calls=%async_computation | async-start | bytes 1048576 | tf_op jit(solution)/shard_map/all_to_all | solution.py:108
  29.3 3.5 copy-start
  34.2 4.4 %copy-start.29 = (bf16[4,128,8,64]{1,3,2,0:T(8,128)(2,1)}, bf16[4,128,8,64]{1,3,2,0:T(8,128)(2,1)S(1)}, u32[]{:S(2)}) copy-start(bf16[4,128,8,64]{1,3,2,0:T(8,128)(2,1)S(1)} %copy.190) | copy-start | bytes 1572868
  38.6 5.6 %copy-start.23 = (bf16[4,128,8,64]{1,3,2,0:T(8,128)(2,1)}, bf16[4,128,8,64]{1,3,2,0:T(8,128)(2,1)S(1)}, u32[]{:S(2)}) copy-start(bf16[4,128,8,64]{1,3,2,0:T(8,128)(2,1)S(1)} %copy.191) | copy-start | bytes 1572868
  44.3 5.5 %copy-start.33 = (bf16[32,16,512]{2,1,0:T(8,128)(2,1)S(1)}, bf16[32,16,512]{2,1,0:T(8,128)(2,1)}, u32[]{:S(2)}) copy-start(bf16[32,16,512]{2,1,0:T(8,128)(2,1)} %param.6) | copy-start | bytes 1572868
  46.3 18.8 %all-to-all-start.1 = ((bf16[4,128,512]{2,0,1:T(4,128)(2,1)}), bf16[4,128,512]{2,0,1:T(4,128)(2,1)S(1)}, u32[]{:S(2)}, u32[]{:S(2)}) async-start(bf16[4,128,512]{2,0,1:T(4,128)(2,1)} %copy.194), calls=%async_computation.1 | async-start | bytes 1048576 | tf_op jit(solution)/shard_map/all_to_all | solution.py:112
  65.0 11.5 %all-to-all-start.4 = ((bf16[32,16,512]{2,0,1:T(8,128)(2,1)}), bf16[32,16,512]{2,0,1:T(8,128)(2,1)S(1)}, u32[]{:S(2)}, u32[]{:S(2)}) async-start(bf16[32,16,512]{2,0,1:T(8,128)(2,1)} %copy.207), calls=%async_computation.4 | async-start | bytes 1048576 | tf_op jit(solution)/shard_map/all_to_all | solution.py:116
  76.6 10.6 %all-to-all-start.2 = ((bf16[32,16,512]{2,0,1:T(8,128)(2,1)}), bf16[32,16,512]{2,0,1:T(8,128)(2,1)S(1)}, u32[]{:S(2)}, u32[]{:S(2)}) async-start(bf16[32,16,512]{2,0,1:T(8,128)(2,1)} %copy.197), calls=%async_computation.2 | async-start | bytes 1048576 | tf_op jit(solution)/shard_map/all_to_all | solution.py:116
  88.2 4.4 %copy-start.2 = (bf16[512,512]{1,0:T(8,128)(2,1)}, bf16[512,512]{1,0:T(8,128)(2,1)S(1)}, u32[]{:S(2)}) copy-start(bf16[512,512]{1,0:T(8,128)(2,1)S(1)} %convert_element_type.216) | copy-start | bytes 1572868
  88.2 4.0 copy-start.15
  102.4 5.3 %copy-start.25 = (bf16[128,4,8,64]{0,3,2,1:T(8,128)(2,1)}, bf16[128,4,8,64]{0,3,2,1:T(8,128)(2,1)S(1)}, u32[]{:S(2)}) copy-start(bf16[128,4,8,64]{0,3,2,1:T(8,128)(2,1)S(1)} %copy.202) | copy-start | bytes 1572868
  112.7 5.1 %copy-start.36 = (bf16[128,4,8,64]{0,3,2,1:T(8,128)(2,1)S(1)}, bf16[128,4,8,64]{0,3,2,1:T(8,128)(2,1)}, u32[]{:S(2)}) copy-start(bf16[128,4,8,64]{0,3,2,1:T(8,128)(2,1)} %fusion.40) | copy-start | bytes 1572868
  148.3 6.2 %copy-start.22 = (bf16[4,8,64,128]{3,2,1,0:T(8,128)(2,1)S(1)}, bf16[4,8,64,128]{3,2,1,0:T(8,128)(2,1)}, u32[]{:S(2)}) copy-start(bf16[4,8,64,128]{3,2,1,0:T(8,128)(2,1)} %copy-done.21) | copy-start | bytes 1572868
  148.3 7.5 %copy-start.26 = (bf16[128,4,8,64]{0,3,2,1:T(8,128)(2,1)S(1)}, bf16[128,4,8,64]{0,3,2,1:T(8,128)(2,1)}, u32[]{:S(2)}) copy-start(bf16[128,4,8,64]{0,3,2,1:T(8,128)(2,1)} %copy-done.25) | copy-start | bytes 1572868
  150.4 11.0 %all-to-all-start.5 = ((bf16[128,4,512]{2,1,0:T(4,128)(2,1)}), bf16[128,4,512]{2,1,0:T(4,128)(2,1)}, u32[]{:S(2)}, u32[]{:S(2)}) async-start(bf16[128,4,512]{2,1,0:T(4,128)(2,1)} %reshape.260), calls=%async_computation.5 | async-start | bytes 1048576 | tf_op jit(solution)/shard_map/all_to_all | solution.py:120
  161.4 6.8 %copy-start.3 = (bf16[512,512]{1,0:T(8,128)(2,1)S(1)}, bf16[512,512]{1,0:T(8,128)(2,1)}, u32[]{:S(2)}) copy-start(bf16[512,512]{1,0:T(8,128)(2,1)} %copy-done.2) | copy-start | bytes 1572868
  163.8 19.5 %all-to-all-start.6 = ((bf16[32,16,512]{2,1,0:T(8,128)(2,1)}), bf16[32,16,512]{2,1,0:T(8,128)(2,1)}, u32[]{:S(2)}, u32[]{:S(2)}) async-start(bf16[32,16,512]{2,1,0:T(8,128)(2,1)} %copy.223), calls=%async_computation.6 | async-start | bytes 1048576 | tf_op jit(solution)/shard_map/all_to_all | solution.py:108
  167.9 229.8 %all-reduce.3.cloned.1.call-start = ((), (), s32[]{:S(2)}) async-start(), calls=%async_computation.8 | async-start | bytes 16777216 | tf_op jit(solution)/shard_map/psum | solution.py:139
  171.5 13.0 %slice-start.1 = ((bf16[4,512,512]{2,1,0:T(8,128)(2,1)}), bf16[1,512,512]{2,1,0:T(8,128)(2,1)S(1)}, s32[]{:S(2)}) async-start(bf16[4,512,512]{2,1,0:T(8,128)(2,1)} %param.7), calls=%async_computation.10 | async-start | bytes 1048576 | tf_op jit(solution)/shard_map/slice | solution.py:55
  193.6 5.2 %copy-start.34 = (bf16[4,128,8,64]{1,3,2,0:T(8,128)(2,1)S(1)}, bf16[4,128,8,64]{1,3,2,0:T(8,128)(2,1)}, u32[]{:S(2)}) copy-start(bf16[4,128,8,64]{1,3,2,0:T(8,128)(2,1)} %fusion.43) | copy-start | bytes 1572868
  207.5 6.9 %copy-start.9 = (bf16[4,128,8,64]{1,0,3,2:T(4,128)(2,1)S(1)}, bf16[4,128,8,64]{1,0,3,2:T(4,128)(2,1)}, u32[]{:S(2)}) copy-start(bf16[4,128,8,64]{1,0,3,2:T(4,128)(2,1)} %copy-done.8) | copy-start | bytes 1572868
  210.2 18.6 %all-to-all-start.3 = ((bf16[128,4,512]{2,1,0:T(4,128)(2,1)}), bf16[128,4,512]{2,1,0:T(4,128)(2,1)S(1)}, u32[]{:S(2)}, u32[]{:S(2)}) async-start(bf16[128,4,512]{2,1,0:T(4,128)(2,1)} %copy.205), calls=%async_computation.3 | async-start | bytes 1048576 | tf_op jit(solution)/shard_map/all_to_all | solution.py:120
  228.8 24.0 %all-to-all-start.7 = ((bf16[4,128,512]{2,0,1:T(4,128)(2,1)}), bf16[4,128,512]{2,0,1:T(4,128)(2,1)S(1)}, u32[]{:S(2)}, u32[]{:S(2)}) async-start(bf16[4,128,512]{2,0,1:T(4,128)(2,1)} %copy.235), calls=%async_computation.7 | async-start | bytes 1048576 | tf_op jit(solution)/shard_map/all_to_all | solution.py:112
  397.8 4.8 %copy-start.14 = (f32[4,512,512]{2,1,0:T(8,128)S(1)}, f32[4,512,512]{2,1,0:T(8,128)}, u32[]{:S(2)}) copy-start(f32[4,512,512]{2,1,0:T(8,128)} %get-tuple-element.19) | copy-start | bytes 12582916
  (26 other events, 47.0 us)
Sparse Core Ops, SparseCore 0:
  205.9 191.7 all-reduce.2
where the time goes:
time: 420 us; the launch traced here: 412 us
  waiting for transfers between devices  220 us (52%)
  local copies, waits for them, and re-layouts  71.8 us (17%)
  matrix products  63.5 us (15%)
  starting transfers between devices  33.4 us (8%)
  between operations  15.2 us (4%)
  other arithmetic  8.12 us (2%)
    psum x1, waiting for transfers between devices, body(): grad_row, grad_col = lax.psum((grad_row, grad_col), ('row', 'col'))  144 us
    all_to_all x2, waiting for transfers between devices, from_rows(): lax.all_to_all(values, 'col', split_axis=1, concat_axis=0, tiled=True)  33.5 us
    all_to_all x2, waiting for transfers between devices, to_rows(): lax.all_to_all(values, 'col', split_axis=0, concat_axis=1, tiled=True)  24 us
    reshape x12, local copies, waits for them, and re-layouts, project(): result.astype(jnp.bfloat16).reshape(in_shape[0], in_shape[1], HEADS, HEAD)  15.2 us
    unnamed x81, local copies, waits for them, and re-layouts  12 us
    all_to_all x2, starting transfers between devices, to_rows(): lax.all_to_all(values, 'col', split_axis=0, concat_axis=1, tiled=True)  10.5 us
    dot_general x2, matrix products, line_backward(): jnp.einsum('nhlm,' + q_spec + '->' + k_spec, grad_scores, q_proj, preferr...  10.3 us
    dot_general x2, matrix products, line_backward(): jnp.einsum('nhlm,' + k_spec + '->' + q_spec, grad_scores, k_proj, preferr...  10.1 us
  transfers between devices with their start and end apart: 9, of which 8 were waited for; matrix products, arithmetic and copies ran while one was open for 7% of the time, Pallas kernels for 0%

commit v1 on v0

v1 whole, which is shorter than its diff:
```python
import functools

import jax
import jax.numpy as jnp
from jax import lax
from jax.experimental import pallas as pl
from jax.experimental.pallas import tpu as pltpu
from jax.sharding import PartitionSpec as P

HEADS = 8
HEAD = 64
EPSILON = 1e-06
BF = jnp.bfloat16
F32 = jnp.float32


def dot(left, right, ca=1, cb=0):
    return lax.dot_general(
        left, right, (((ca,), (cb,)), ((), ())), preferred_element_type=F32
    )


def reorder(rows, sizes, order):
    total = rows.shape[0]
    index = lax.broadcasted_iota(jnp.int32, (total, 1), 0)
    strides, stride = [0] * len(sizes), 1
    for axis in reversed(range(len(sizes))):
        strides[axis], stride = stride, stride * sizes[axis]
    source, stride = jnp.zeros_like(index), 1
    for axis in reversed(order):
        digit = lax.rem(lax.div(index, jnp.int32(stride)), jnp.int32(sizes[axis]))
        source = source + digit * strides[axis]
        stride *= sizes[axis]
    column = lax.broadcasted_iota(jnp.int32, (total, total), 1)
    matrix = jnp.where(column == source, 1.0, 0.0).astype(BF)
    return dot(matrix, rows).astype(BF)


def inverse_rms(values):
    return lax.rsqrt(jnp.mean(values * values, axis=-1, keepdims=True) + EPSILON)


def halves(pair, first):
    zero = jnp.zeros_like(pair)
    return jnp.concatenate([jnp.where(first, pair, zero), jnp.where(first, zero, pair)], axis=0)


def attention(lines, q_ref, k_ref, v_ref, a_ref, da_ref, dq_ref, dk_ref, dv_ref, gain_ref):
    length = q_ref.shape[0] // lines
    wide = 2 * HEAD
    first = lax.broadcasted_iota(jnp.int32, (length, wide), 1) < HEAD
    scale = HEAD ** (-0.5)

    def line(which, carry):
        rows = pl.ds(pl.multiple_of(which * length, length), length)
        for pair in range(HEADS // 2):
            lanes = slice(pair * wide, (pair + 1) * wide)
            q, k, v = q_ref[rows, lanes], k_ref[rows, lanes], v_ref[rows, lanes]
            k2, v2 = halves(k, first), halves(v, first)
            scores = dot(q, k2, 1, 1) * scale
            probs = []
            for part in (scores[:, :length], scores[:, length:]):
                e = jnp.exp(part - jnp.max(part, axis=-1, keepdims=True))
                probs.append(e * (1.0 / jnp.sum(e, axis=-1, keepdims=True)))
            low = jnp.concatenate([x.astype(BF) for x in probs], axis=1)
            if a_ref is not None:
                a_ref[rows, lanes] = (dot(low, v2) * gain_ref[:, lanes]).astype(BF)
            if da_ref is not None:
                da = da_ref[rows, lanes]
                dp = dot(da, v2, 1, 1)
                ds = []
                for x, y in zip(probs, (dp[:, :length], dp[:, length:])):
                    xy = x * y
                    mean = jnp.sum(xy, axis=-1, keepdims=True)
                    ds.append(((xy - x * mean) * scale).astype(BF))
                ds = jnp.concatenate(ds, axis=1)
                dq_ref[rows, lanes] = dot(ds, k2).astype(BF)
                dk = dot(ds, q, 0, 0)
                dk_ref[rows, lanes] = jnp.where(first, dk[:length], dk[length:]).astype(BF)
                dv = dot(low, da, 0, 0)
                dv_ref[rows, lanes] = jnp.where(first, dv[:length], dv[length:]).astype(BF)
        return carry

    lax.fori_loop(0, lines, line, 0)


def input_grad(g, u, dq_ref, dk_ref, dv_ref, w_ref):
    dn = dot(dq_ref[...], w_ref[0], 1, 1) + dot(dk_ref[...], w_ref[1], 1, 1)
    dn = dn + dot(dv_ref[...], w_ref[2], 1, 1)
    uf = u.astype(F32)
    r = inverse_rms(uf)
    mean = jnp.mean(dn * uf, axis=-1, keepdims=True)
    return (g.astype(F32) + r * (dn - uf * (r * r * mean))).astype(BF)


def weight_grads(dw_ref, n_ref, a_ref, g_ref, dq_ref, dk_ref, dv_ref):
    for i, (left, right) in enumerate(
        ((n_ref, dq_ref), (n_ref, dk_ref), (n_ref, dv_ref), (a_ref, g_ref))
    ):
        dw_ref[i] = dot(left[...], right[...], 0, 0).astype(dw_ref.dtype)


def row_forward(cfg, x_ref, w_ref, gain_ref, mid_ref, u_ref, n_ref, q_ref, k_ref, v_ref, a_ref):
    nr, nc, ri, cj = cfg
    ct = nr * cj
    u_ref[...] = reorder(x_ref[...], (nc, ri, ct), (1, 0, 2))
    uf = u_ref[...].astype(F32)
    n_ref[...] = (uf * inverse_rms(uf)).astype(BF)
    for i, ref in enumerate((q_ref, k_ref, v_ref)):
        ref[...] = dot(n_ref[...], w_ref[i]).astype(BF)
    attention(ri, q_ref, k_ref, v_ref, a_ref, None, None, None, None, gain_ref)
    mid = (u_ref[...].astype(F32) + dot(a_ref[...], w_ref[3])).astype(BF)
    mid_ref[...] = reorder(mid, (ri, nc, nr, cj), (2, 1, 3, 0))


def column(cfg, x_ref, c_ref, w_ref, gain_ref, out_ref, dmid_ref, dw_ref,
           u_ref, g_ref, n_ref, q_ref, k_ref, v_ref, a_ref, da_ref, dq_ref, dk_ref, dv_ref):
    nr, nc, ri, cj = cfg
    rt = nc * ri
    g_ref[...] = reorder(c_ref[...], (nr, cj, rt), (1, 0, 2))
    da_ref[...] = (dot(g_ref[...], w_ref[3], 1, 1) * gain_ref[...]).astype(BF)
    u_ref[...] = reorder(x_ref[...], (nr * nc, cj, ri), (1, 0, 2))
    uf = u_ref[...].astype(F32)
    n_ref[...] = (uf * inverse_rms(uf)).astype(BF)
    for i, ref in enumerate((q_ref, k_ref, v_ref)):
        ref[...] = dot(n_ref[...], w_ref[i]).astype(BF)
    attention(cj, q_ref, k_ref, v_ref, a_ref, da_ref, dq_ref, dk_ref, dv_ref, gain_ref)
    dmid = input_grad(g_ref[...], u_ref[...], dq_ref, dk_ref, dv_ref, w_ref)
    dmid_ref[...] = reorder(dmid, (cj, nr * nc, ri), (1, 0, 2))
    out = (u_ref[...].astype(F32) + dot(a_ref[...], w_ref[3])).astype(BF)
    out_ref[...] = reorder(out, (cj, nr, rt), (1, 0, 2))
    weight_grads(dw_ref, n_ref, a_ref, g_ref, dq_ref, dk_ref, dv_ref)


def row_backward(cfg, d_ref, w_ref, gain_ref, u_ref, n_ref, q_ref, k_ref, v_ref, a_ref,
                 gin_ref, dw_ref, g_ref, da_ref, dq_ref, dk_ref, dv_ref):
    nr, nc, ri, cj = cfg
    ct = nr * cj
    g_ref[...] = reorder(d_ref[...], (nr, nc, cj, ri), (3, 1, 0, 2))
    da_ref[...] = (dot(g_ref[...], w_ref[3], 1, 1) * gain_ref[...]).astype(BF)
    attention(ri, q_ref, k_ref, v_ref, None, da_ref, dq_ref, dk_ref, dv_ref, gain_ref)
    gin = input_grad(g_ref[...], u_ref[...], dq_ref, dk_ref, dv_ref, w_ref)
    gin_ref[...] = reorder(gin, (ri, nc, ct), (1, 0, 2))
    weight_grads(dw_ref, n_ref, a_ref, g_ref, dq_ref, dk_ref, dv_ref)


def call(kernel, name, n_in, outs, scratch, flops):
    vmem = pl.BlockSpec(memory_space=pltpu.VMEM)
    return pl.pallas_call(
        kernel,
        name=name,
        out_shape=outs,
        in_specs=[vmem] * n_in,
        out_specs=[vmem] * len(outs),
        scratch_shapes=scratch,
        compiler_params=pltpu.CompilerParams(vmem_limit_bytes=40 * 2**20),
        cost_estimate=pl.CostEstimate(flops=flops, bytes_accessed=6 * 2**20, transcendentals=0),
    )


def body(sizes, latents, cotangent, w_row, w_col, keep_heads):
    nr, nc = sizes
    rt, ct, width = latents.shape
    ri, cj = rt // nc, ct // nr
    cfg = (nr, nc, ri, cj)
    tokens = rt * ct
    flat = (tokens, width)
    gains = jnp.repeat(keep_heads.astype(F32), HEAD, axis=1)
    gain_row, gain_col = gains[:1], gains[1:]
    act = jax.ShapeDtypeStruct(flat, BF)
    dw = jax.ShapeDtypeStruct(w_row.shape, BF)
    tile = pltpu.VMEM(flat, BF)
    unit = 2 * tokens * width * width

    def exchange(values, axes, parts):
        pieces = values.reshape(parts, tokens // parts, width)
        return lax.all_to_all(pieces, axes, split_axis=0, concat_axis=0, tiled=True).reshape(flat)

    x_rows = exchange(latents, "col", nc)
    g_cols = exchange(cotangent.transpose(1, 0, 2), "row", nr)
    mid, *saved = call(
        functools.partial(row_forward, cfg), "row_forward", 3, [act] * 7, [], 6 * unit
    )(x_rows, w_row, gain_row)
    x_cols = exchange(mid, ("row", "col"), nr * nc)
    out, dmid, dw_col = call(
        functools.partial(column, cfg), "column", 4, [act, act, dw], [tile] * 11, 16 * unit
    )(x_cols, g_cols, w_col, gain_col)
    g_rows = exchange(dmid, ("row", "col"), nr * nc)
    grad_col = lax.psum(dw_col, ("row", "col")).astype(F32)
    output = exchange(out, "row", nr).reshape(ct, rt, width).transpose(1, 0, 2)
    gin, dw_row = call(
        functools.partial(row_backward, cfg), "row_backward", 9, [act, dw], [tile] * 5, 12 * unit
    )(g_rows, w_row, gain_row, *saved)
    dw_row, grad_col = lax.optimization_barrier((dw_row, grad_col))
    grad_row = lax.psum(dw_row, ("row", "col")).astype(F32)
    grad_latents = exchange(gin, "col", nc).reshape(latents.shape)
    return (output, grad_latents, grad_row, grad_col)


def solution(mesh):
    in_specs = (P("row", "col", None), P("row", "col", None), P(), P(), P())
    out_specs = (P("row", "col", None), P("row", "col", None), P(), P())
    sizes = (mesh.shape["row"], mesh.shape["col"])
    return jax.shard_map(
        functools.partial(body, sizes), mesh=mesh, in_specs=in_specs, out_specs=out_specs,
        check_vma=False,
    )
```

time: 420 us -> 383 us (0.912); the launches traced: 412 us -> 382 us
  matrix products: 63.5 us -> 0 us
  waiting for transfers between devices: 220 us -> 283 us
  local copies, waits for them, and re-layouts: 71.8 us -> 17 us
  Pallas kernels: 0 us -> 35.3 us
  starting transfers between devices: 33.4 us -> 24.7 us
    psum x1 -> x2, waiting for transfers between devices: 144 us -> 219 us  [the longest x1 117 us: body(): grad_row = lax.psum(dw_row, ('row', 'col')).astype(F32)]
    dot_general x34 -> x0, matrix products: 57.8 us -> none  [the longest x2 10.3 us: line_backward(): jnp.einsum('nhlm,' + q_spec + '->' + k_spec, grad_scores, q_proj, preferr...]
    pallas_call x0 -> x3, Pallas kernels: none -> 35.3 us  [the longest x1 15.7 us: body(): call(functools.partial(column, cfg), 'column', 4, [act, act, dw], [tile]...]
    reshape x19 -> x0, local copies, waits for them, and re-layouts: 28.8 us -> none  [the longest x12 15.2 us: project(): result.astype(jnp.bfloat16).reshape(in_shape[0], in_shape[1], HEADS, HEAD)]
    convert_element_type x16 -> x0, local copies, waits for them, and re-layouts: 22.6 us -> none  [the longest x2 4.98 us: line_backward(): grad_k = grad_k.astype(jnp.bfloat16).reshape(-1, model_width)]
    all_to_all x8 -> x6, waiting for transfers between devices: 75.8 us -> 62.6 us  [exchange(): lax.all_to_all(pieces, axes, split_axis=0, concat_axis=0, tiled=True)]
    all_to_all x8 -> x6, starting transfers between devices: 33.1 us -> 24.4 us  [exchange(): lax.all_to_all(pieces, axes, split_axis=0, concat_axis=0, tiled=True)]
    all_to_all x12 -> x0, local copies, waits for them, and re-layouts: 8.11 us -> none  [the longest x5 3.52 us: from_cols(): lax.all_to_all(values, 'row', split_axis=0, concat_axis=1, tiled=True)]
  transfers between devices with their start and end apart: 9 -> 8, of which waited for: 8 -> 6; matrix products, arithmetic and copies ran while one was open for 7% -> 2% of each run, Pallas kernels for 0% -> 5%
where the time goes in v1:
time: 383 us; the launch traced here: 382 us
  waiting for transfers between devices  283 us (74%)
  Pallas kernels  35.3 us (9%)
  starting transfers between devices  24.7 us (6%)
  local copies, waits for them, and re-layouts  17 us (4%)
  between operations  14.1 us (4%)
  other arithmetic  8.39 us (2%)
    psum x1, waiting for transfers between devices, body(): grad_row = lax.psum(dw_row, ('row', 'col')).astype(F32)  117 us
    psum x1, waiting for transfers between devices, body(): grad_col = lax.psum(dw_col, ('row', 'col')).astype(F32)  103 us
    all_to_all x6, waiting for transfers between devices, exchange(): lax.all_to_all(pieces, axes, split_axis=0, concat_axis=0, tiled=True)  62.6 us
    all_to_all x6, starting transfers between devices, exchange(): lax.all_to_all(pieces, axes, split_axis=0, concat_axis=0, tiled=True)  24.4 us
    unnamed x35, local copies, waits for them, and re-layouts  16.7 us
    pallas_call x1, Pallas kernels, body(): call(functools.partial(column, cfg), 'column', 4, [act, act, dw], [tile]...  15.7 us
    pallas_call x1, Pallas kernels, body(): call(functools.partial(row_backward, cfg), 'row_backward', 9, [act, dw],...  13.1 us
  transfers between devices with their start and end apart: 8, of which 6 were waited for; matrix products, arithmetic and copies ran while one was open for 2% of the time, Pallas kernels for 5%

profile of v1, /device:TPU:0, one launch (start us, length us, event | category | flops | bytes accessed | tf_op | source)
XLA Modules:
  0.0 382.1 jit_solution(1488699753746076813)
XLA Ops:
  7.2 6.3 %all-to-all-start = ((bf16[8,64,512]{2,1,0:T(8,128)(2,1)}), bf16[8,64,512]{2,1,0:T(8,128)(2,1)S(1)}, u32[]{:S(2)}, u32[]{:S(2)}) async-start(bf16[8,64,512]{2,1,0:T(8,128)(2,1)} %bitcast.25), calls=%async_computation | async-start | bytes 1048576 | tf_op jit(solution)/shard_map/all_to_all | solution.py:177
  13.5 2.1 copy.9
  15.6 13.2 %all-to-all-done = bf16[8,64,512]{2,1,0:T(8,128)(2,1)S(1)} async-done(((bf16[8,64,512]{2,1,0:T(8,128)(2,1)}), bf16[8,64,512]{2,1,0:T(8,128)(2,1)S(1)}, u32[]{:S(2)}, u32[]{:S(2)}) %all-to-all-start) | async-done | bytes 524320 | tf_op jit(solution)/shard_map/all_to_all | solution.py:177
  28.9 3.7 all-to-all-start.2
  32.8 1.6 copy-done.1
  34.3 6.5 %row_forward.1 = (bf16[512,512]{1,0:T(8,128)(2,1)}, bf16[512,512]{1,0:T(8,128)(2,1)S(1)}, bf16[512,512]{1,0:T(8,128)(2,1)S(1)}, bf16[512,512]{1,0:T(8,128)(2,1)S...) custom-call(bf16[512,512]{1,0:T(8,128)(2,1)S(1)} %bitcast.22, ...), custom_call_target="tpu_custom_call" | custom-call | flops 1610612736 | bytes 6291456 | tf_op jit(solution)/shard_map/row_forward/pallas_call | solution.py:181
  45.7 4.0 %all-to-all-start.1 = ((bf16[32,16,512]{2,1,0:T(8,128)(2,1)}), bf16[32,16,512]{2,1,0:T(8,128)(2,1)S(1)}, u32[]{:S(2)}, u32[]{:S(2)}) async-start(bf16[32,16,512]{2,1,0:T(8,128)(2,1)} %bitcast.3), calls=%async_computation.1 | async-start | bytes 1048576 | tf_op jit(solution)/shard_map/all_to_all | solution.py:177
  49.8 16.2 %all-to-all-done.1 = bf16[32,16,512]{2,1,0:T(8,128)(2,1)S(1)} async-done(((bf16[32,16,512]{2,1,0:T(8,128)(2,1)}), bf16[32,16,512]{2,1,0:T(8,128)(2,1)S(1)}, u32[]{:S(2)}, u32[]{:S(2)}) %all-to-all-start.1) | async-done | bytes 524320 | tf_op jit(solution)/shard_map/all_to_all | solution.py:177
  66.0 15.7 %column.1 = (bf16[512,512]{1,0:T(8,128)(2,1)}, bf16[512,512]{1,0:T(8,128)(2,1)}, bf16[4,512,512]{2,1,0:T(8,128)(2,1)}) custom-call(bf16[512,512]{1,0:T(8,128)(2,1)S(1)} %bitcast.23, bf16[512,512]{1,0:T(8,128)(2,1)S(1)} %bitcast.20, bf16[4,512,512]{2,1,0:T(8,128)(2,1)S(1)} %copy-done, f32[1,512]{1,0:T(1,128)S(1)} %broadcast_in_dim.12.gain_ref), custom_call_target="tpu_custom_call" | custom-call | flops 4294967296 | bytes 6291456 | tf_op jit(solution)/shard_map/column/pallas_call | solution.py:185
  81.8 2.8 all-to-all-start.4
  85.3 15.6 %all-to-all-done.4 = bf16[32,16,512]{2,1,0:T(8,128)(2,1)S(1)} async-done(((bf16[32,16,512]{2,1,0:T(8,128)(2,1)}), bf16[32,16,512]{2,1,0:T(8,128)(2,1)S(1)}, u32[]{:S(2)}, u32[]{:S(2)}) %all-to-all-start.4) | async-done | bytes 524320 | tf_op jit(solution)/shard_map/all_to_all | solution.py:177
  100.9 4.1 %all-to-all-start.3 = ((bf16[4,128,512]{2,1,0:T(8,128)(2,1)}), bf16[4,128,512]{2,1,0:T(8,128)(2,1)}, u32[]{:S(2)}, u32[]{:S(2)}) async-start(bf16[4,128,512]{2,1,0:T(8,128)(2,1)} %bitcast.9), calls=%async_computation.3 | async-start | bytes 1048576 | tf_op jit(solution)/shard_map/all_to_all | solution.py:177
  106.3 1.0 copy-done.8
  107.4 1.0 copy-done.10
  108.4 1.0 copy-done.12
  109.5 1.0 copy-done.14
  110.5 13.1 %row_backward.1 = (bf16[512,512]{1,0:T(8,128)(2,1)}, bf16[4,512,512]{2,1,0:T(8,128)(2,1)}) custom-call(bf16[512,512]{1,0:T(8,128)(2,1)S(1)} %bitcast.21, bf16[4,512,512]{2,1,0:T(8,128)(2,1)S(1)} %copy-done.2, f32[1,512]{1,0:T(1,128)S(1)} %broadcast_in_dim.10.gain_ref, bf16[512,512]{1,0:T(8,128)(2,1)S(1)} %copy-done.4, bf16[512,512]{1,0:T(8,128)(2,1)S(1)} %copy-done.6, ...), custom_call_target="tpu_custom_call" | custom-call | flops 3221225472 | bytes 6291456 | tf_op jit(solution)/shard_map/row_backward/pallas_call | solution.py:191
  123.6 102.7 %all-reduce.3.cloned.1.call-done = bf16[4,512,512]{2,1,0:T(8,128)(2,1)} async-done(((bf16[4,512,512]{2,1,0:T(8,128)(2,1)}), bf16[4,512,512]{2,1,0:T(8,128)(2,1)}) %all-reduce.3.cloned.1.call-update) | async-done | bytes 2097168 | tf_op jit(solution)/shard_map/psum | solution.py:189
  226.3 4.2 %convert_element_type.10 = f32[4,512,512]{2,1,0:T(8,128)} convert(bf16[4,512,512]{2,1,0:T(8,128)(2,1)} %all-reduce.3.cloned.1.call-done) | non-fusion elementwise | flops 1048576 | bytes 6291456 | tf_op jit(solution)/shard_map/convert_element_type | solution.py:189
  230.6 3.5 all-to-all-start.5
  234.1 2.1 copy.10
  236.2 17.5 %all-to-all-done.5 = bf16[8,64,512]{2,1,0:T(8,128)(2,1)S(1)} async-done(((bf16[8,64,512]{2,1,0:T(8,128)(2,1)}), bf16[8,64,512]{2,1,0:T(8,128)(2,1)S(1)}, u32[]{:S(2)}, u32[]{:S(2)}) %all-to-all-start.5) | async-done | bytes 524320 | tf_op jit(solution)/shard_map/all_to_all | solution.py:177
  253.7 116.6 %all-reduce.5.cloned.1.call-done = bf16[4,512,512]{2,1,0:T(8,128)(2,1)} async-done(((bf16[4,512,512]{2,1,0:T(8,128)(2,1)}), bf16[4,512,512]{2,1,0:T(8,128)(2,1)}) %all-reduce.5.cloned.1.call-update) | async-done | bytes 2097168 | tf_op jit(solution)/shard_map/psum | solution.py:195
  370.3 4.2 %convert_element_type.11 = f32[4,512,512]{2,1,0:T(8,128)} convert(bf16[4,512,512]{2,1,0:T(8,128)(2,1)} %all-reduce.5.cloned.1.call-done) | non-fusion elementwise | flops 1048576 | bytes 6291456 | tf_op jit(solution)/shard_map/convert_element_type | solution.py:195
  (40 shorter events, 7.9 us)
Async XLA Ops:
  7.2 25.4 %copy-start.15 = (s32[2,8]{1,0:T(2,128)S(1)}, s32[2,8]{1,0:T(2,128)}, u32[]{:S(2)}) copy-start(s32[2,8]{1,0:T(2,128)} %param.9) | copy-start | bytes 196
  7.2 21.7 %all-to-all-start = ((bf16[8,64,512]{2,1,0:T(8,128)(2,1)}), bf16[8,64,512]{2,1,0:T(8,128)(2,1)S(1)}, u32[]{:S(2)}, u32[]{:S(2)}) async-start(bf16[8,64,512]{2,1,0:T(8,128)(2,1)} %bitcast.25), calls=%async_computation | async-start | bytes 1048576 | tf_op jit(solution)/shard_map/all_to_all | solution.py:177
  28.9 16.8 %all-to-all-start.2 = ((bf16[4,128,512]{2,1,0:T(8,128)(2,1)}), bf16[4,128,512]{2,1,0:T(8,128)(2,1)S(1)}, u32[]{:S(2)}, u32[]{:S(2)}) async-start(bf16[4,128,512]{2,1,0:T(8,128)(2,1)} %bitcast.6), calls=%async_computation.2 | async-start | bytes 1048576 | tf_op jit(solution)/shard_map/all_to_all | solution.py:177
  32.8 1.6 copy-start.1
  34.3 31.7 %copy-start = (bf16[4,512,512]{2,1,0:T(8,128)(2,1)S(1)}, bf16[4,512,512]{2,1,0:T(8,128)(2,1)}, u32[]{:S(2)}) copy-start(bf16[4,512,512]{2,1,0:T(8,128)(2,1)} %w_ref.4) | copy-start | bytes 6291460
  40.9 0.8 copy-start.3
  41.7 0.8 copy-start.5
  42.5 0.8 copy-start.7
  43.3 0.8 copy-start.9
  44.1 0.8 copy-start.11
  44.9 0.8 copy-start.13
  45.7 20.3 %all-to-all-start.1 = ((bf16[32,16,512]{2,1,0:T(8,128)(2,1)}), bf16[32,16,512]{2,1,0:T(8,128)(2,1)S(1)}, u32[]{:S(2)}, u32[]{:S(2)}) async-start(bf16[32,16,512]{2,1,0:T(8,128)(2,1)} %bitcast.3), calls=%async_computation.1 | async-start | bytes 1048576 | tf_op jit(solution)/shard_map/all_to_all | solution.py:177
  81.8 23.5 %copy-start.2 = (bf16[4,512,512]{2,1,0:T(8,128)(2,1)S(1)}, bf16[4,512,512]{2,1,0:T(8,128)(2,1)}, u32[]{:S(2)}) copy-start(bf16[4,512,512]{2,1,0:T(8,128)(2,1)} %w_ref.5) | copy-start | bytes 6291460
  81.8 23.5 %copy-start.4 = (bf16[512,512]{1,0:T(8,128)(2,1)S(1)}, bf16[512,512]{1,0:T(8,128)(2,1)}, u32[]{:S(2)}) copy-start(bf16[512,512]{1,0:T(8,128)(2,1)} %copy-done.3) | copy-start | bytes 1572868
  81.8 19.1 %all-to-all-start.4 = ((bf16[32,16,512]{2,1,0:T(8,128)(2,1)}), bf16[32,16,512]{2,1,0:T(8,128)(2,1)S(1)}, u32[]{:S(2)}, u32[]{:S(2)}) async-start(bf16[32,16,512]{2,1,0:T(8,128)(2,1)} %bitcast.12), calls=%async_computation.4 | async-start | bytes 1048576 | tf_op jit(solution)/shard_map/all_to_all | solution.py:177
  84.5 141.8 %all-reduce.3.cloned.1.call-start = ((), (), s32[]{:S(2)}) async-start(), calls=%async_computation.6 | async-start | bytes 4194304 | tf_op jit(solution)/shard_map/psum | solution.py:189
  100.9 129.7 %all-to-all-start.3 = ((bf16[4,128,512]{2,1,0:T(8,128)(2,1)}), bf16[4,128,512]{2,1,0:T(8,128)(2,1)}, u32[]{:S(2)}, u32[]{:S(2)}) async-start(bf16[4,128,512]{2,1,0:T(8,128)(2,1)} %bitcast.9), calls=%async_computation.3 | async-start | bytes 1048576 | tf_op jit(solution)/shard_map/all_to_all | solution.py:177
  105.0 265.2 %all-reduce.5.cloned.1.call-start = ((), (), s32[]{:S(2)}) async-start(), calls=%async_computation.7 | async-start | bytes 4194304 | tf_op jit(solution)/shard_map/psum | solution.py:195
  105.3 1.0 copy-start.6
  106.3 1.0 copy-start.8
  107.4 1.0 copy-start.10
  108.4 1.0 copy-start.12
  109.5 1.0 copy-start.14
  230.6 23.1 %all-to-all-start.5 = ((bf16[8,64,512]{2,1,0:T(8,128)(2,1)}), bf16[8,64,512]{2,1,0:T(8,128)(2,1)S(1)}, u32[]{:S(2)}, u32[]{:S(2)}) async-start(bf16[8,64,512]{2,1,0:T(8,128)(2,1)} %bitcast.14), calls=%async_computation.5 | async-start | bytes 1048576 | tf_op jit(solution)/shard_map/all_to_all | solution.py:177
Sparse Core Ops, SparseCore 0:
  91.3 134.9 all-reduce.2
  233.1 137.1 all-reduce.4

commit v2 on v1

--- a/solution.py
+++ b/solution.py
@@ -144,6 +144,141 @@
     weight_grads(dw_ref, n_ref, a_ref, g_ref, dq_ref, dk_ref, dv_ref)
 
 
+def sum_kernel(nr, nc, parts, col_ref, row_ref, out_ref, land0, work0, land1, work1, land2,
+               send_sem, recv_sem):
+    r, c = lax.axis_index("row"), lax.axis_index("col")
+    nz = nc // 2
+    z, core = c // 2, lax.rem(c, 2)
+    rows = out_ref.shape[0] // parts
+    half = rows // 2
+    rc = half // nr
+    zc = rc // nz
+    pair = (r, z * 2 + (1 - core))
+    row_peer = [(lax.rem(r + d, nr), c) for d in range(1, nr)]
+    z_peer = [(r, lax.rem(z + d, nz) * 2 + core) for d in range(1, nz)]
+    peers = [pair] + row_peer + z_peer
+
+    barrier = pltpu.get_barrier_semaphore()
+    for peer in peers:
+        pl.semaphore_signal(barrier, inc=1, device_id=peer, device_id_type=pl.DeviceIdType.MESH)
+    pl.semaphore_wait(barrier, len(peers))
+
+    def span(start, size):
+        return pl.ds(pl.multiple_of(start, 16), size)
+
+    def copy(part, slot, source, target, peer):
+        made = pltpu.make_async_remote_copy(
+            src_ref=source, dst_ref=target, send_sem=send_sem.at[part, slot],
+            recv_sem=recv_sem.at[part, slot], device_id=peer,
+            device_id_type=pl.DeviceIdType.MESH,
+        )
+        made.start()
+        return made
+
+    def add(size, sources, store):
+        step = min(size, 64)
+        while size % step:
+            step -= 16
+
+        def one(i, carry):
+            at = i * step
+            total = sources[0](at, step).astype(F32)
+            for source in sources[1:]:
+                total = total + source(at, step).astype(F32)
+            store(at, step, total.astype(BF))
+            return carry
+
+        lax.fori_loop(0, size // step, one, 0)
+
+    def reader(ref, base, *lead):
+        return lambda at, step: ref[(*lead, span(base + at, step), slice(None))]
+
+    def writer(ref, base, *lead):
+        def store(at, step, value):
+            ref[(*lead, span(base + at, step), slice(None))] = value
+
+        return store
+
+    def run(part):
+        own, local = (col_ref, part) if part < parts // 2 else (row_ref, part - parts // 2)
+        start = local * rows
+        other = [copy(part, 0, own.at[span(start + (1 - core) * half, half)], land0.at[part], pair)]
+        yield other
+        add(half, [reader(own, start + core * half), reader(land0, 0, part)],
+            writer(work0, 0, part))
+        slot = 1
+        made = []
+        for d, peer in enumerate(row_peer):
+            made.append(copy(part, slot, work0.at[part, span(peer[0] * rc, rc)],
+                             land1.at[part, d], peer))
+            slot += 1
+        yield made
+        add(rc, [reader(work0, r * rc, part)] + [reader(land1, 0, part, d) for d in range(nr - 1)],
+            writer(work1, 0, part))
+        made = []
+        for d, peer in enumerate(z_peer):
+            to = lax.rem(z + d + 1, nz)
+            made.append(copy(part, slot, work1.at[part, span(to * zc, zc)],
+                             land2.at[part, d], peer))
+            slot += 1
+        yield made
+        base0 = part * rows + core * half
+        base1 = base0 + r * rc
+        base2 = base1 + z * zc
+        add(zc, [reader(work1, z * zc, part)] + [reader(land2, 0, part, d) for d in range(nz - 1)],
+            writer(out_ref, base2))
+        for base, size, group in ((base2, zc, z_peer), (base1, rc, row_peer), (base0, half, [pair])):
+            made = []
+            for peer in group:
+                block = out_ref.at[span(base, size)]
+                made.append(copy(part, slot, block, block, peer))
+                slot += 1
+            yield made
+
+    runs = [run(part) for part in range(parts)]
+    flying = [next(x) for x in runs]
+    for stage in range(6):
+        for i, x in enumerate(runs):
+            for made in flying[i]:
+                made.wait()
+            flying[i] = next(x, [])
+
+
+def all_sum(sizes, dw_col, dw_row):
+    nr, nc = sizes
+    shape, width = dw_col.shape, dw_col.shape[2]
+    rows = 2 * shape[0] * shape[1]
+    parts = 4 if rows % (4 * nr * nc * 16) == 0 else 2
+    half = rows // parts // 2
+    rc = half // nr
+    nz = nc // 2
+    zc = rc // nz
+    vmem = pl.BlockSpec(memory_space=pltpu.VMEM)
+    slots = 2 * (1 + nr - 1 + nz - 1)
+    total = pl.pallas_call(
+        functools.partial(sum_kernel, nr, nc, parts),
+        name="all_sum",
+        out_shape=jax.ShapeDtypeStruct((rows, width), BF),
+        in_specs=[vmem, vmem],
+        out_specs=vmem,
+        scratch_shapes=[
+            pltpu.VMEM((parts, half, width), BF),
+            pltpu.VMEM((parts, half, width), BF),
+            pltpu.VMEM((parts, nr - 1, rc, width), BF),
+            pltpu.VMEM((parts, rc, width), BF),
+            pltpu.VMEM((parts, nz - 1, zc, width), BF),
+            pltpu.SemaphoreType.DMA((parts, slots)),
+            pltpu.SemaphoreType.DMA((parts, slots)),
+        ],
+        compiler_params=pltpu.CompilerParams(
+            collective_id=0, has_side_effects=True, vmem_limit_bytes=40 * 2**20
+        ),
+        cost_estimate=pl.CostEstimate(flops=10**9, bytes_accessed=200 * 2**20, transcendentals=0),
+    )(dw_col.reshape(-1, width), dw_row.reshape(-1, width))
+    total = total.reshape((2,) + shape)
+    return total[1].astype(F32), total[0].astype(F32)
+
+
 def call(kernel, name, n_in, outs, scratch, flops):
     vmem = pl.BlockSpec(memory_space=pltpu.VMEM)
     return pl.pallas_call(
@@ -186,14 +321,12 @@
         functools.partial(column, cfg), "column", 4, [act, act, dw], [tile] * 11, 16 * unit
     )(x_cols, g_cols, w_col, gain_col)
     g_rows = exchange(dmid, ("row", "col"), nr * nc)
-    grad_col = lax.psum(dw_col, ("row", "col")).astype(F32)
     output = exchange(out, "row", nr).reshape(ct, rt, width).transpose(1, 0, 2)
     gin, dw_row = call(
         functools.partial(row_backward, cfg), "row_backward", 9, [act, dw], [tile] * 5, 12 * unit
     )(g_rows, w_row, gain_row, *saved)
-    dw_row, grad_col = lax.optimization_barrier((dw_row, grad_col))
-    grad_row = lax.psum(dw_row, ("row", "col")).astype(F32)
     grad_latents = exchange(gin, "col", nc).reshape(latents.shape)
+    grad_row, grad_col = all_sum(sizes, dw_col, dw_row)
     return (output, grad_latents, grad_row, grad_col)
 
 

time: 383 us -> 196 us (0.51)
  waiting for transfers between devices: 283 us -> 29.4 us
  Pallas kernels: 35.3 us -> 96.3 us
  blocking collectives: 0 us -> 18.4 us
  between operations: 14.1 us -> 0.75 us
  local copies, waits for them, and re-layouts: 17 us -> 23.3 us
    psum x2 -> x0, waiting for transfers between devices: 219 us -> none  [the longest x1 117 us: body(): grad_row = lax.psum(dw_row, ('row', 'col')).astype(F32)]
    pallas_call x0 -> x1, Pallas kernels: none -> 63.7 us  [all_sum(): pl.pallas_call(functools.partial(sum_kernel, nr, nc, parts), name='all_su...]
    all_to_all x6 -> x5, waiting for transfers between devices: 62.6 us -> 29.4 us  [exchange(): lax.all_to_all(pieces, axes, split_axis=0, concat_axis=0, tiled=True)]
    all_to_all x0 -> x1, blocking collectives: none -> 18.4 us  [exchange(): lax.all_to_all(pieces, axes, split_axis=0, concat_axis=0, tiled=True)]
    unnamed x35 -> x39, local copies, waits for them, and re-layouts: 16.7 us -> 22.7 us
    all_to_all x6 -> x5, starting transfers between devices: 24.4 us -> 21.8 us  [exchange(): lax.all_to_all(pieces, axes, split_axis=0, concat_axis=0, tiled=True)]
  transfers between devices with their start and end apart: 8 -> 5, of which waited for: 6 -> 2; matrix products, arithmetic and copies ran while one was open for 2% -> 5% of each run, Pallas kernels for 5% -> 42%
where the time goes in v2:
time: 196 us; the launch traced here: 195 us
  Pallas kernels  96.3 us (49%)
  waiting for transfers between devices  29.4 us (15%)
  local copies, waits for them, and re-layouts  23.3 us (12%)
  starting transfers between devices  21.8 us (11%)
  blocking collectives  18.4 us (9%)
  other arithmetic  5.21 us (3%)
    pallas_call x1, Pallas kernels, all_sum(): pl.pallas_call(functools.partial(sum_kernel, nr, nc, parts), name='all_su...  63.7 us
    all_to_all x5, waiting for transfers between devices, exchange(): lax.all_to_all(pieces, axes, split_axis=0, concat_axis=0, tiled=True)  29.4 us
    unnamed x39, local copies, waits for them, and re-layouts  22.7 us
    all_to_all x5, starting transfers between devices, exchange(): lax.all_to_all(pieces, axes, split_axis=0, concat_axis=0, tiled=True)  21.8 us
    all_to_all x1, blocking collectives, exchange(): lax.all_to_all(pieces, axes, split_axis=0, concat_axis=0, tiled=True)  18.4 us
    pallas_call x1, Pallas kernels, body(): call(functools.partial(column, cfg), 'column', 4, [act, act, dw], [tile]...  14.4 us
    pallas_call x1, Pallas kernels, body(): call(functools.partial(row_backward, cfg), 'row_backward', 9, [act, dw],...  11.8 us
    pallas_call x1, Pallas kernels, body(): call(functools.partial(row_forward, cfg), 'row_forward', 3, [act] * 7, []...  6.54 us
  transfers between devices with their start and end apart: 5, of which 2 were waited for; matrix products, arithmetic and copies ran while one was open for 5% of the time, Pallas kernels for 42%

profile of v2, /device:TPU:0, one launch (start us, length us, event | category | flops | bytes accessed | tf_op | source)
XLA Modules:
  0.0 195.3 jit_solution(1233157456972683499)
XLA Ops:
  0.6 6.3 %all-to-all-start = ((bf16[8,64,512]{2,1,0:T(8,128)(2,1)}), bf16[8,64,512]{2,1,0:T(8,128)(2,1)S(1)}, u32[]{:S(2)}, u32[]{:S(2)}) async-start(bf16[8,64,512]{2,1,0:T(8,128)(2,1)} %bitcast.36), calls=%async_computation | async-start | bytes 1048576 | tf_op jit(solution)/shard_map/all_to_all | solution.py:312
  7.0 2.1 %copy.9 = bf16[32,16,512]{2,0,1:T(8,128)(2,1)} copy(bf16[32,16,512]{2,1,0:T(8,128)(2,1)} %param.6) | data formatting | bytes 1048576 | tf_op args[1]
  9.1 13.2 %all-to-all-done = bf16[8,64,512]{2,1,0:T(8,128)(2,1)S(1)} async-done(((bf16[8,64,512]{2,1,0:T(8,128)(2,1)}), bf16[8,64,512]{2,1,0:T(8,128)(2,1)S(1)}, u32[]{:S(2)}, u32[]{:S(2)}) %all-to-all-start) | async-done | bytes 524320 | tf_op jit(solution)/shard_map/all_to_all | solution.py:312
  22.3 3.7 %all-to-all-start.2 = ((bf16[4,128,512]{2,1,0:T(8,128)(2,1)}), bf16[4,128,512]{2,1,0:T(8,128)(2,1)S(1)}, u32[]{:S(2)}, u32[]{:S(2)}) async-start(bf16[4,128,512]{2,1,0:T(8,128)(2,1)} %bitcast.6), calls=%async_computation.2 | async-start | bytes 1048576 | tf_op jit(solution)/shard_map/all_to_all | solution.py:312
  26.2 1.6 copy-done.3
  27.8 6.5 %row_forward.1 = (bf16[512,512]{1,0:T(8,128)(2,1)}, bf16[512,512]{1,0:T(8,128)(2,1)S(1)}, bf16[512,512]{1,0:T(8,128)(2,1)S(1)}, bf16[512,512]{1,0:T(8,128)(2,1)S...) custom-call(bf16[512,512]{1,0:T(8,128)(2,1)S(1)} %bitcast.29, ...), custom_call_target="tpu_custom_call" | custom-call | flops 1610612736 | bytes 6291456 | tf_op jit(solution)/shard_map/row_forward/pallas_call | solution.py:316
  39.2 4.0 %all-to-all-start.1 = ((bf16[32,16,512]{2,1,0:T(8,128)(2,1)}), bf16[32,16,512]{2,1,0:T(8,128)(2,1)S(1)}, u32[]{:S(2)}, u32[]{:S(2)}) async-start(bf16[32,16,512]{2,1,0:T(8,128)(2,1)} %bitcast.3), calls=%async_computation.1 | async-start | bytes 1048576 | tf_op jit(solution)/shard_map/all_to_all | solution.py:312
  43.3 16.2 %all-to-all-done.1 = bf16[32,16,512]{2,1,0:T(8,128)(2,1)S(1)} async-done(((bf16[32,16,512]{2,1,0:T(8,128)(2,1)}), bf16[32,16,512]{2,1,0:T(8,128)(2,1)S(1)}, u32[]{:S(2)}, u32[]{:S(2)}) %all-to-all-start.1) | async-done | bytes 524320 | tf_op jit(solution)/shard_map/all_to_all | solution.py:312
  59.5 1.6 copy-done.2
  61.1 14.4 %column.1 = (bf16[512,512]{1,0:T(8,128)(2,1)}, bf16[512,512]{1,0:T(8,128)(2,1)S(1)}, bf16[4,512,512]{2,1,0:T(8,128)(2,1)S(1)}) custom-call(bf16[512,512]{1,0:T(8,128)(2,1)S(1)} %bitcast.30, bf16[512,512]{1,0:T(8,128)(2,1)S(1)} %bitcast.28, bf16[4,512,512]{2,1,0:T(8,128)(2,1)S(1)} %copy-done.2, f32[1,512]{1,0:T(1,128)S(1)} %broadcast_in_dim.12.gain_ref), custom_call_target="tpu_custom_call" | custom-call | flops 4294967296 | bytes 6291456 | tf_op jit(solution)/shard_map/column/pallas_call | solution.py:320
  75.5 18.4 %all_to_all.30 = bf16[32,16,512]{2,1,0:T(8,128)(2,1)S(1)} all-to-all(bf16[32,16,512]{2,1,0:T(8,128)(2,1)S(1)} %bitcast.32), channel_id=1, replica_groups=mesh['row'=4,'col'=8] {'row','col'}, dimensions={0} | all-to-all | bytes 1048576 | tf_op jit(solution)/shard_map/all_to_all | solution.py:312
  93.9 4.3 %all-to-all-start.3 = ((bf16[4,128,512]{2,1,0:T(8,128)(2,1)}), bf16[4,128,512]{2,1,0:T(8,128)(2,1)}, u32[]{:S(2)}, u32[]{:S(2)}) async-start(bf16[4,128,512]{2,1,0:T(8,128)(2,1)} %bitcast.9), calls=%async_computation.3 | async-start | bytes 1048576 | tf_op jit(solution)/shard_map/all_to_all | solution.py:312
  98.2 1.6 copy-done.4
  99.8 1.0 copy-done.8
  101.9 1.0 copy-done.12
  102.9 1.0 copy-done.14
  105.0 11.8 %row_backward.1 = (bf16[512,512]{1,0:T(8,128)(2,1)}, bf16[4,512,512]{2,1,0:T(8,128)(2,1)S(1)}) custom-call(bf16[512,512]{1,0:T(8,128)(2,1)S(1)} %bitcast.31, bf16[4,512,512]{2,1,0:T(8,128)(2,1)S(1)} %copy-done.4, f32[1,512]{1,0:T(1,128)S(1)} %broadcast_in_dim.10.gain_ref, bf16[512,512]{1,0:T(8,128)(2,1)S(1)} %copy-done.6, bf16[512,512]{1,0:T(8,128)(2,1)S(1)} %copy-done.8, ...), custom_call_target="tpu_custom_call" | custom-call | flops 3221225472 | bytes 6291456 | tf_op jit(solution)/shard_map/row_backward/pallas_call | solution.py:325
  116.8 1.3 copy-done
  118.1 3.5 %all-to-all-start.5 = ((bf16[8,64,512]{2,1,0:T(8,128)(2,1)}), bf16[8,64,512]{2,1,0:T(8,128)(2,1)S(1)}, u32[]{:S(2)}, u32[]{:S(2)}) async-start(bf16[8,64,512]{2,1,0:T(8,128)(2,1)} %bitcast.14), calls=%async_computation.5 | async-start | bytes 1048576 | tf_op jit(solution)/shard_map/all_to_all | solution.py:312
  121.6 2.1 %copy.10 = bf16[32,16,512]{2,1,0:T(8,128)(2,1)} copy(bf16[32,16,512]{2,0,1:T(8,128)(2,1)} %bitcast.11) | data formatting | bytes 1048576
  123.7 1.6 copy-done.1
  125.3 63.7 %all_sum.1 = bf16[4096,512]{1,0:T(8,128)(2,1)S(1)} custom-call(bf16[2048,512]{1,0:T(8,128)(2,1)S(1)} %bitcast.26, bf16[2048,512]{1,0:T(8,128)(2,1)S(1)} %bitcast.27), custom_call_target="tpu_custom_call" | custom-call | flops 1000000000 | bytes 209715200 | tf_op jit(solution)/shard_map/all_sum/pallas_call | solution.py:258
  189.3 2.6 %convert.2 = f32[4,512,512]{2,1,0:T(8,128)} convert(bf16[4,512,512]{2,1,0:T(8,128)(2,1)S(1)} %bitcast.34) | non-fusion elementwise | flops 1048576 | bytes 6291456 | tf_op jit(solution)/shard_map/convert_element_type | solution.py:279
  191.9 2.6 %convert.3 = f32[4,512,512]{2,1,0:T(8,128)} convert(bf16[4,512,512]{2,1,0:T(8,128)(2,1)S(1)} %bitcast.33) | non-fusion elementwise | flops 1048576 | bytes 6291456 | tf_op jit(solution)/shard_map/convert_element_type | solution.py:279
  (39 shorter events, 8.3 us)
Async XLA Ops:
  0.6 25.4 %copy-start.17 = (s32[2,8]{1,0:T(2,128)S(1)}, s32[2,8]{1,0:T(2,128)}, u32[]{:S(2)}) copy-start(s32[2,8]{1,0:T(2,128)} %param.9) | copy-start | bytes 196
  0.6 21.7 %all-to-all-start = ((bf16[8,64,512]{2,1,0:T(8,128)(2,1)}), bf16[8,64,512]{2,1,0:T(8,128)(2,1)S(1)}, u32[]{:S(2)}, u32[]{:S(2)}) async-start(bf16[8,64,512]{2,1,0:T(8,128)(2,1)} %bitcast.36), calls=%async_computation | async-start | bytes 1048576 | tf_op jit(solution)/shard_map/all_to_all | solution.py:312
  22.3 16.8 %all-to-all-start.2 = ((bf16[4,128,512]{2,1,0:T(8,128)(2,1)}), bf16[4,128,512]{2,1,0:T(8,128)(2,1)S(1)}, u32[]{:S(2)}, u32[]{:S(2)}) async-start(bf16[4,128,512]{2,1,0:T(8,128)(2,1)} %bitcast.6), calls=%async_computation.2 | async-start | bytes 1048576 | tf_op jit(solution)/shard_map/all_to_all | solution.py:312
  26.2 1.6 copy-start.3
  34.4 0.8 copy-start.5
  35.1 0.8 copy-start.7
  35.9 0.8 copy-start.9
  36.8 0.8 copy-start.11
  37.6 0.8 copy-start.13
  38.4 0.8 copy-start.15
  39.2 20.3 %all-to-all-start.1 = ((bf16[32,16,512]{2,1,0:T(8,128)(2,1)}), bf16[32,16,512]{2,1,0:T(8,128)(2,1)S(1)}, u32[]{:S(2)}, u32[]{:S(2)}) async-start(bf16[32,16,512]{2,1,0:T(8,128)(2,1)} %bitcast.3), calls=%async_computation.1 | async-start | bytes 1048576 | tf_op jit(solution)/shard_map/all_to_all | solution.py:312
  59.5 1.6 copy-start.2
  75.5 22.7 %copy-start.6 = (bf16[512,512]{1,0:T(8,128)(2,1)S(1)}, bf16[512,512]{1,0:T(8,128)(2,1)}, u32[]{:S(2)}) copy-start(bf16[512,512]{1,0:T(8,128)(2,1)} %copy-done.5) | copy-start | bytes 1572868
  93.9 24.2 %all-to-all-start.3 = ((bf16[4,128,512]{2,1,0:T(8,128)(2,1)}), bf16[4,128,512]{2,1,0:T(8,128)(2,1)}, u32[]{:S(2)}, u32[]{:S(2)}) async-start(bf16[4,128,512]{2,1,0:T(8,128)(2,1)} %bitcast.9), calls=%async_computation.3 | async-start | bytes 1048576 | tf_op jit(solution)/shard_map/all_to_all | solution.py:312
  98.2 1.6 copy-start.4
  99.8 1.0 copy-start.8
  100.9 1.0 copy-start.10
  101.9 1.0 copy-start.12
  102.9 1.0 copy-start.14
  104.0 1.0 copy-start.16
  116.8 1.3 copy-start
  118.1 76.4 %all-to-all-start.5 = ((bf16[8,64,512]{2,1,0:T(8,128)(2,1)}), bf16[8,64,512]{2,1,0:T(8,128)(2,1)S(1)}, u32[]{:S(2)}, u32[]{:S(2)}) async-start(bf16[8,64,512]{2,1,0:T(8,128)(2,1)} %bitcast.14), calls=%async_computation.5 | async-start | bytes 1048576 | tf_op jit(solution)/shard_map/all_to_all | solution.py:312
  123.7 1.6 copy-start.1

commit v3 on v2

--- a/solution.py
+++ b/solution.py
@@ -97,10 +97,11 @@
     for i, (left, right) in enumerate(
         ((n_ref, dq_ref), (n_ref, dk_ref), (n_ref, dv_ref), (a_ref, g_ref))
     ):
-        dw_ref[i] = dot(left[...], right[...], 0, 0).astype(dw_ref.dtype)
-
-
-def row_forward(cfg, x_ref, w_ref, gain_ref, mid_ref, u_ref, n_ref, q_ref, k_ref, v_ref, a_ref):
+        width = left.shape[1]
+        dw_ref[i * width:(i + 1) * width, :] = dot(left[...], right[...], 0, 0).astype(BF)
+
+
+def row_forward(cfg, x_ref, w_ref, gain_ref, mid_ref, u_ref, a_ref, n_ref, q_ref, k_ref, v_ref):
     nr, nc, ri, cj = cfg
     ct = nr * cj
     u_ref[...] = reorder(x_ref[...], (nc, ri, ct), (1, 0, 2))
@@ -132,20 +133,12 @@
     weight_grads(dw_ref, n_ref, a_ref, g_ref, dq_ref, dk_ref, dv_ref)
 
 
-def row_backward(cfg, d_ref, w_ref, gain_ref, u_ref, n_ref, q_ref, k_ref, v_ref, a_ref,
-                 gin_ref, dw_ref, g_ref, da_ref, dq_ref, dk_ref, dv_ref):
+def finish(cfg, parts, d_ref, col_ref, w_ref, gain_ref, u_ref, a_ref, out_ref, glat_ref, row_ref, n_ref, q_ref, k_ref, v_ref,
+            hop1, turned, hop2, gin_ref, g_ref, da_ref, dq_ref, dk_ref,
+           dv_ref, land0, work0, land1, work1, land2, send_sem, recv_sem, hop1_sem, hop2_sem,
+           gin_sem):
     nr, nc, ri, cj = cfg
-    ct = nr * cj
-    g_ref[...] = reorder(d_ref[...], (nr, nc, cj, ri), (3, 1, 0, 2))
-    da_ref[...] = (dot(g_ref[...], w_ref[3], 1, 1) * gain_ref[...]).astype(BF)
-    attention(ri, q_ref, k_ref, v_ref, None, da_ref, dq_ref, dk_ref, dv_ref, gain_ref)
-    gin = input_grad(g_ref[...], u_ref[...], dq_ref, dk_ref, dv_ref, w_ref)
-    gin_ref[...] = reorder(gin, (ri, nc, ct), (1, 0, 2))
-    weight_grads(dw_ref, n_ref, a_ref, g_ref, dq_ref, dk_ref, dv_ref)
-
-
-def sum_kernel(nr, nc, parts, col_ref, row_ref, out_ref, land0, work0, land1, work1, land2,
-               send_sem, recv_sem):
+    tokens = d_ref.shape[0]
     r, c = lax.axis_index("row"), lax.axis_index("col")
     nz = nc // 2
     z, core = c // 2, lax.rem(c, 2)
@@ -155,8 +148,9 @@
     zc = rc // nz
     pair = (r, z * 2 + (1 - core))
     row_peer = [(lax.rem(r + d, nr), c) for d in range(1, nr)]
+    col_peer = [(r, lax.rem(c + d, nc)) for d in range(1, nc)]
     z_peer = [(r, lax.rem(z + d, nz) * 2 + core) for d in range(1, nz)]
-    peers = [pair] + row_peer + z_peer
+    peers = row_peer + col_peer
 
     barrier = pltpu.get_barrier_semaphore()
     for peer in peers:
@@ -235,18 +229,74 @@
                 slot += 1
             yield made
 
-    runs = [run(part) for part in range(parts)]
-    flying = [next(x) for x in runs]
-    for stage in range(6):
-        for i, x in enumerate(runs):
-            for made in flying[i]:
-                made.wait()
-            flying[i] = next(x, [])
-
-
-def all_sum(sizes, dw_col, dw_row):
-    nr, nc = sizes
-    shape, width = dw_col.shape, dw_col.shape[2]
+    def exchange(source, target, size, mine, group, axis, sems):
+        made = []
+        for d, peer in enumerate(group):
+            copied = pltpu.make_async_remote_copy(
+                src_ref=source.at[span(peer[axis] * size, size)],
+                dst_ref=target.at[span(mine * size, size)],
+                send_sem=sems.at[0, d], recv_sem=sems.at[1, d], device_id=peer,
+                device_id_type=pl.DeviceIdType.MESH,
+            )
+            copied.start()
+            made.append(copied)
+        target[span(mine * size, size), :] = source[span(mine * size, size), :]
+        return made
+
+    def finished(made):
+        for copied in made:
+            copied.wait()
+
+    flying = {}
+
+    def begin(part):
+        steps = run(part)
+        flying[part] = (steps, next(steps))
+
+    def advance(which):
+        for part in which:
+            steps, made = flying[part]
+            finished(made)
+            flying[part] = (steps, next(steps, []))
+
+    cols, later = range(parts // 2), range(parts // 2, parts)
+    made = exchange(d_ref, hop1, tokens // nr, r, row_peer, 0, hop1_sem)
+    for part in cols:
+        begin(part)
+    uf = u_ref[...].astype(F32)
+    n_ref[...] = (uf * inverse_rms(uf)).astype(BF)
+    for i, ref in enumerate((q_ref, k_ref, v_ref)):
+        ref[...] = dot(n_ref[...], w_ref[i]).astype(BF)
+    finished(made)
+    turned[...] = reorder(hop1[...], (nr, nc, cj * ri), (1, 0, 2))
+    made = exchange(turned, hop2, tokens // nc, c, col_peer, 1, hop2_sem)
+    advance(cols)
+    finished(made)
+    g_ref[...] = reorder(hop2[...], (nc, nr, cj, ri), (3, 0, 1, 2))
+    da_ref[...] = (dot(g_ref[...], w_ref[3], 1, 1) * gain_ref[...]).astype(BF)
+    advance(cols)
+    attention(ri, q_ref, k_ref, v_ref, None, da_ref, dq_ref, dk_ref, dv_ref, gain_ref)
+    weight_grads(row_ref, n_ref, a_ref, g_ref, dq_ref, dk_ref, dv_ref)
+    advance(cols)
+    for part in later:
+        begin(part)
+    gin = input_grad(g_ref[...], u_ref[...], dq_ref, dk_ref, dv_ref, w_ref)
+    gin_ref[...] = reorder(gin, (ri, nc, nr * cj), (1, 0, 2))
+    advance(later)
+    advance(cols)
+    made = exchange(gin_ref, glat_ref, tokens // nc, c, col_peer, 1, gin_sem)
+    advance(later)
+    advance(cols)
+    advance(later)
+    advance(cols)
+    for _ in range(3):
+        advance(later)
+    finished(made)
+
+
+def last_kernel(cfg, dmid, dw_col, w_row, gain_row, saved):
+    nr, nc = cfg[:2]
+    shape, width = w_row.shape, w_row.shape[2]
     rows = 2 * shape[0] * shape[1]
     parts = 4 if rows % (4 * nr * nc * 16) == 0 else 2
     half = rows // parts // 2
@@ -255,13 +305,16 @@
     zc = rc // nz
     vmem = pl.BlockSpec(memory_space=pltpu.VMEM)
     slots = 2 * (1 + nr - 1 + nz - 1)
-    total = pl.pallas_call(
-        functools.partial(sum_kernel, nr, nc, parts),
-        name="all_sum",
-        out_shape=jax.ShapeDtypeStruct((rows, width), BF),
-        in_specs=[vmem, vmem],
-        out_specs=vmem,
+    tile = pltpu.VMEM(dmid.shape, BF)
+    total, glat = pl.pallas_call(
+        functools.partial(finish, cfg, parts),
+        name="finish",
+        out_shape=[jax.ShapeDtypeStruct((rows, width), BF), jax.ShapeDtypeStruct(dmid.shape, BF)],
+        in_specs=[vmem] * 6,
+        out_specs=[vmem] * 2,
         scratch_shapes=[
+            pltpu.VMEM((rows // 2, width), BF),
+        ] + [tile] * 13 + [
             pltpu.VMEM((parts, half, width), BF),
             pltpu.VMEM((parts, half, width), BF),
             pltpu.VMEM((parts, nr - 1, rc, width), BF),
@@ -269,14 +322,17 @@
             pltpu.VMEM((parts, nz - 1, zc, width), BF),
             pltpu.SemaphoreType.DMA((parts, slots)),
             pltpu.SemaphoreType.DMA((parts, slots)),
+            pltpu.SemaphoreType.DMA((2, nr - 1)),
+            pltpu.SemaphoreType.DMA((2, nc - 1)),
+            pltpu.SemaphoreType.DMA((2, nc - 1)),
         ],
         compiler_params=pltpu.CompilerParams(
-            collective_id=0, has_side_effects=True, vmem_limit_bytes=40 * 2**20
+            collective_id=0, has_side_effects=True, vmem_limit_bytes=36 * 2**20
         ),
         cost_estimate=pl.CostEstimate(flops=10**9, bytes_accessed=200 * 2**20, transcendentals=0),
-    )(dw_col.reshape(-1, width), dw_row.reshape(-1, width))
+    )(dmid, dw_col, w_row, gain_row, *saved)
     total = total.reshape((2,) + shape)
-    return total[1].astype(F32), total[0].astype(F32)
+    return total[1].astype(F32), total[0].astype(F32), glat
 
 
 def call(kernel, name, n_in, outs, scratch, flops):
@@ -288,7 +344,7 @@
         in_specs=[vmem] * n_in,
         out_specs=[vmem] * len(outs),
         scratch_shapes=scratch,
-        compiler_params=pltpu.CompilerParams(vmem_limit_bytes=40 * 2**20),
+        compiler_params=pltpu.CompilerParams(vmem_limit_bytes=24 * 2**20),
         cost_estimate=pl.CostEstimate(flops=flops, bytes_accessed=6 * 2**20, transcendentals=0),
     )
 
@@ -303,7 +359,7 @@
     gains = jnp.repeat(keep_heads.astype(F32), HEAD, axis=1)
     gain_row, gain_col = gains[:1], gains[1:]
     act = jax.ShapeDtypeStruct(flat, BF)
-    dw = jax.ShapeDtypeStruct(w_row.shape, BF)
+    dw = jax.ShapeDtypeStruct((w_row.shape[0] * width, width), BF)
     tile = pltpu.VMEM(flat, BF)
     unit = 2 * tokens * width * width
 
@@ -314,19 +370,15 @@
     x_rows = exchange(latents, "col", nc)
     g_cols = exchange(cotangent.transpose(1, 0, 2), "row", nr)
     mid, *saved = call(
-        functools.partial(row_forward, cfg), "row_forward", 3, [act] * 7, [], 6 * unit
+        functools.partial(row_forward, cfg), "row_forward", 3, [act] * 3, [tile] * 4, 6 * unit
     )(x_rows, w_row, gain_row)
     x_cols = exchange(mid, ("row", "col"), nr * nc)
     out, dmid, dw_col = call(
         functools.partial(column, cfg), "column", 4, [act, act, dw], [tile] * 11, 16 * unit
     )(x_cols, g_cols, w_col, gain_col)
-    g_rows = exchange(dmid, ("row", "col"), nr * nc)
     output = exchange(out, "row", nr).reshape(ct, rt, width).transpose(1, 0, 2)
-    gin, dw_row = call(
-        functools.partial(row_backward, cfg), "row_backward", 9, [act, dw], [tile] * 5, 12 * unit
-    )(g_rows, w_row, gain_row, *saved)
-    grad_latents = exchange(gin, "col", nc).reshape(latents.shape)
-    grad_row, grad_col = all_sum(sizes, dw_col, dw_row)
+    grad_row, grad_col, glat = last_kernel(cfg, dmid, dw_col, w_row, gain_row, saved)
+    grad_latents = glat.reshape(latents.shape)
     return (output, grad_latents, grad_row, grad_col)
 
 

time: 196 us -> 169 us (0.86)
  blocking collectives: 18.4 us -> 0 us
  local copies, waits for them, and re-layouts: 23.3 us -> 15.4 us
  starting transfers between devices: 21.8 us -> 17.8 us
  Pallas kernels: 96.3 us -> 99.5 us
    all_to_all x1 -> x0, blocking collectives: 18.4 us -> none  [exchange(): lax.all_to_all(pieces, axes, split_axis=0, concat_axis=0, tiled=True)]
    unnamed x39 -> x27, local copies, waits for them, and re-layouts: 22.7 us -> 14.8 us
    all_to_all x5 -> x4, starting transfers between devices: 21.8 us -> 17.8 us  [exchange(): lax.all_to_all(pieces, axes, split_axis=0, concat_axis=0, tiled=True)]
    pallas_call x3 -> x2, Pallas kernels: 82 us -> 85.1 us  [the longest x1 79.4 us: last_kernel(): pl.pallas_call(functools.partial(finish, cfg, parts), name='finish', out_...]
    all_to_all x5 -> x4, waiting for transfers between devices: 29.4 us -> 29.4 us  [exchange(): lax.all_to_all(pieces, axes, split_axis=0, concat_axis=0, tiled=True)]
  transfers between devices with their start and end apart: 5 -> 4, of which waited for: 2 -> 2; matrix products, arithmetic and copies ran while one was open for 5% -> 5% of each run, Pallas kernels for 42% -> 51%
where the time goes in v3:
time: 169 us; the launch traced here: 168 us
  Pallas kernels  99.5 us (59%)
  waiting for transfers between devices  29.4 us (17%)
  starting transfers between devices  17.8 us (11%)
  local copies, waits for them, and re-layouts  15.4 us (9%)
  other arithmetic  5.21 us (3%)
    pallas_call x1, Pallas kernels, last_kernel(): pl.pallas_call(functools.partial(finish, cfg, parts), name='finish', out_...  79.4 us
    all_to_all x4, waiting for transfers between devices, exchange(): lax.all_to_all(pieces, axes, split_axis=0, concat_axis=0, tiled=True)  29.4 us
    all_to_all x4, starting transfers between devices, exchange(): lax.all_to_all(pieces, axes, split_axis=0, concat_axis=0, tiled=True)  17.8 us
    unnamed x27, local copies, waits for them, and re-layouts  14.8 us
    pallas_call x1, Pallas kernels, body(): call(functools.partial(column, cfg), 'column', 4, [act, act, dw], [tile]...  14.4 us
    pallas_call x1, Pallas kernels, body(): call(functools.partial(row_forward, cfg), 'row_forward', 3, [act] * 3, [t...  5.71 us
    convert_element_type x2, other arithmetic, last_kernel(): return (total[1].astype(F32), total[0].astype(F32), glat)  5.2 us
  transfers between devices with their start and end apart: 4, of which 2 were waited for; matrix products, arithmetic and copies ran while one was open for 5% of the time, Pallas kernels for 51%

profile of v3, /device:TPU:0, one launch (start us, length us, event | category | flops | bytes accessed | tf_op | source)
XLA Modules:
  0.0 168.1 jit_solution(1984737601850133051)
XLA Ops:
  0.7 6.5 %all-to-all-start = ((bf16[8,64,512]{2,1,0:T(8,128)(2,1)}), bf16[8,64,512]{2,1,0:T(8,128)(2,1)S(1)}, u32[]{:S(2)}, u32[]{:S(2)}) async-start(bf16[8,64,512]{2,1,0:T(8,128)(2,1)} %bitcast.30), calls=%async_computation | async-start | bytes 1048576 | tf_op jit(solution)/shard_map/all_to_all | solution.py:368
  7.1 2.1 %copy.9 = bf16[32,16,512]{2,0,1:T(8,128)(2,1)} copy(bf16[32,16,512]{2,1,0:T(8,128)(2,1)} %param.6) | data formatting | bytes 1048576 | tf_op args[1]
  9.2 13.2 %all-to-all-done = bf16[8,64,512]{2,1,0:T(8,128)(2,1)S(1)} async-done(((bf16[8,64,512]{2,1,0:T(8,128)(2,1)}), bf16[8,64,512]{2,1,0:T(8,128)(2,1)S(1)}, u32[]{:S(2)}, u32[]{:S(2)}) %all-to-all-start) | async-done | bytes 524320 | tf_op jit(solution)/shard_map/all_to_all | solution.py:368
  22.5 3.7 %all-to-all-start.2 = ((bf16[4,128,512]{2,1,0:T(8,128)(2,1)}), bf16[4,128,512]{2,1,0:T(8,128)(2,1)S(1)}, u32[]{:S(2)}, u32[]{:S(2)}) async-start(bf16[4,128,512]{2,1,0:T(8,128)(2,1)} %bitcast.29), calls=%async_computation.2 | async-start | bytes 1048576 | tf_op jit(solution)/shard_map/all_to_all | solution.py:368
  26.4 5.7 %row_forward.1 = (bf16[512,512]{1,0:T(8,128)(2,1)S(1)}, bf16[512,512]{1,0:T(8,128)(2,1)S(1)}, bf16[512,512]{1,0:T(8,128)(2,1)S(1)}) custom-call(bf16[512,512]{1,0:T(8,128)(2,1)S(1)} %bitcast.22, bf16[4,512,512]{2,1,0:T(8,128)(2,1)S(1)} %copy-done, f32[1,512]{1,0:T(1,128)S(1)} %broadcast_in_dim.10.gain_ref), custom_call_target="tpu_custom_call" | custom-call | flops 1610612736 | bytes 6291456 | tf_op jit(solution)/shard_map/row_forward/pallas_call | solution.py:372
  32.1 0.8 copy-done.3
  32.9 0.8 copy-done.4
  33.7 0.8 copy-done.6
  34.5 4.0 %all-to-all-start.1 = ((bf16[32,16,512]{2,1,0:T(8,128)(2,1)}), bf16[32,16,512]{2,1,0:T(8,128)(2,1)S(1)}, u32[]{:S(2)}, u32[]{:S(2)}) async-start(bf16[32,16,512]{2,1,0:T(8,128)(2,1)} %bitcast.24), calls=%async_computation.1 | async-start | bytes 1048576 | tf_op jit(solution)/shard_map/all_to_all | solution.py:368
  38.6 16.2 %all-to-all-done.1 = bf16[32,16,512]{2,1,0:T(8,128)(2,1)S(1)} async-done(((bf16[32,16,512]{2,1,0:T(8,128)(2,1)}), bf16[32,16,512]{2,1,0:T(8,128)(2,1)S(1)}, u32[]{:S(2)}, u32[]{:S(2)}) %all-to-all-start.1) | async-done | bytes 524320 | tf_op jit(solution)/shard_map/all_to_all | solution.py:368
  54.8 1.6 copy-done.10
  56.4 14.4 %column.1 = (bf16[512,512]{1,0:T(8,128)(2,1)}, bf16[512,512]{1,0:T(8,128)(2,1)S(1)}, bf16[2048,512]{1,0:T(8,128)(2,1)S(1)}) custom-call(bf16[512,512]{1,0:T(8,128)(2,1)S(1)} %bitcast.25, bf16[512,512]{1,0:T(8,128)(2,1)S(1)} %bitcast.21, bf16[4,512,512]{2,1,0:T(8,128)(2,1)S(1)} %copy-done.10, f32[1,512]{1,0:T(1,128)S(1)} %broadcast_in_dim.12.gain_ref), custom_call_target="tpu_custom_call" | custom-call | flops 4294967296 | bytes 6291456 | tf_op jit(solution)/shard_map/column/pallas_call | solution.py:376
  70.8 1.3 copy-done.1
  72.1 0.8 copy-done.8
  72.9 3.7 %all-to-all-start.3 = ((bf16[4,128,512]{2,1,0:T(8,128)(2,1)}), bf16[4,128,512]{2,1,0:T(8,128)(2,1)S(1)}, u32[]{:S(2)}, u32[]{:S(2)}) async-start(bf16[4,128,512]{2,1,0:T(8,128)(2,1)} %bitcast.9), calls=%async_computation.3 | async-start | bytes 1048576 | tf_op jit(solution)/shard_map/all_to_all | solution.py:368
  76.6 1.6 copy-done.2
  78.2 1.0 copy-done.5
  79.2 1.0 copy-done.7
  80.3 1.0 copy-done.9
  81.3 79.4 %finish.1 = (bf16[4096,512]{1,0:T(8,128)(2,1)S(1)}, bf16[512,512]{1,0:T(8,128)(2,1)S(1)}) custom-call(bf16[512,512]{1,0:T(8,128)(2,1)S(1)} %copy-done.9, bf16[2048,512]{1,0:T(8,128)(2,1)S(1)} %copy-done.2, bf16[4,512,512]{2,1,0:T(8,128)(2,1)S(1)} %copy-done, f32[1,512]{1,0:T(1,128)S(1)} %broadcast_in_dim.10.gain_ref, bf16[512,512]{1,0:T(8,128)(2,1)S(1)} %copy-done.5, ...), custom_call_target="tpu_custom_call" | custom-call | flops 1000000000 | bytes 209715200 | tf_op jit(solution)/shard_map/finish/pallas_call | solution.py:309
  161.0 2.6 %convert.2 = f32[4,512,512]{2,1,0:T(8,128)} convert(bf16[4,512,512]{2,1,0:T(8,128)(2,1)S(1)} %bitcast.27) | non-fusion elementwise | flops 1048576 | bytes 6291456 | tf_op jit(solution)/shard_map/convert_element_type | solution.py:335
  163.6 2.6 %convert.3 = f32[4,512,512]{2,1,0:T(8,128)} convert(bf16[4,512,512]{2,1,0:T(8,128)(2,1)S(1)} %bitcast.26) | non-fusion elementwise | flops 1048576 | bytes 6291456 | tf_op jit(solution)/shard_map/convert_element_type | solution.py:335
  166.2 1.1 copy.10
  167.3 0.8 copy.12
  (23 shorter events, 0.6 us)
Async XLA Ops:
  0.6 25.6 %copy-start.11 = (s32[2,8]{1,0:T(2,128)S(1)}, s32[2,8]{1,0:T(2,128)}, u32[]{:S(2)}) copy-start(s32[2,8]{1,0:T(2,128)} %param.9) | copy-start | bytes 196
  0.6 25.7 %copy-start = (bf16[4,512,512]{2,1,0:T(8,128)(2,1)S(1)}, bf16[4,512,512]{2,1,0:T(8,128)(2,1)}, u32[]{:S(2)}) copy-start(bf16[4,512,512]{2,1,0:T(8,128)(2,1)} %w_ref.5) | copy-start | bytes 6291460
  0.7 21.8 %all-to-all-start = ((bf16[8,64,512]{2,1,0:T(8,128)(2,1)}), bf16[8,64,512]{2,1,0:T(8,128)(2,1)S(1)}, u32[]{:S(2)}, u32[]{:S(2)}) async-start(bf16[8,64,512]{2,1,0:T(8,128)(2,1)} %bitcast.30), calls=%async_computation | async-start | bytes 1048576 | tf_op jit(solution)/shard_map/all_to_all | solution.py:368
  22.5 12.0 %all-to-all-start.2 = ((bf16[4,128,512]{2,1,0:T(8,128)(2,1)}), bf16[4,128,512]{2,1,0:T(8,128)(2,1)S(1)}, u32[]{:S(2)}, u32[]{:S(2)}) async-start(bf16[4,128,512]{2,1,0:T(8,128)(2,1)} %bitcast.29), calls=%async_computation.2 | async-start | bytes 1048576 | tf_op jit(solution)/shard_map/all_to_all | solution.py:368
  32.1 0.8 copy-start.3
  32.9 0.8 copy-start.4
  33.7 0.8 copy-start.6
  34.5 20.4 %all-to-all-start.1 = ((bf16[32,16,512]{2,1,0:T(8,128)(2,1)}), bf16[32,16,512]{2,1,0:T(8,128)(2,1)S(1)}, u32[]{:S(2)}, u32[]{:S(2)}) async-start(bf16[32,16,512]{2,1,0:T(8,128)(2,1)} %bitcast.24), calls=%async_computation.1 | async-start | bytes 1048576 | tf_op jit(solution)/shard_map/all_to_all | solution.py:368
  54.8 1.6 copy-start.10
  70.8 1.3 copy-start.1
  72.1 0.8 copy-start.8
  72.9 93.3 %all-to-all-start.3 = ((bf16[4,128,512]{2,1,0:T(8,128)(2,1)}), bf16[4,128,512]{2,1,0:T(8,128)(2,1)S(1)}, u32[]{:S(2)}, u32[]{:S(2)}) async-start(bf16[4,128,512]{2,1,0:T(8,128)(2,1)} %bitcast.9), calls=%async_computation.3 | async-start | bytes 1048576 | tf_op jit(solution)/shard_map/all_to_all | solution.py:368
  76.6 1.6 copy-start.2
  78.2 1.0 copy-start.5
  79.2 1.0 copy-start.7
  80.3 1.0 copy-start.9

commit v4 on v3

--- a/solution.py
+++ b/solution.py
@@ -101,33 +101,75 @@
         dw_ref[i * width:(i + 1) * width, :] = dot(left[...], right[...], 0, 0).astype(BF)
 
 
-def row_forward(cfg, x_ref, w_ref, gain_ref, mid_ref, u_ref, a_ref, n_ref, q_ref, k_ref, v_ref):
+def greet(peers):
+    barrier = pltpu.get_barrier_semaphore()
+    for peer in peers:
+        pl.semaphore_signal(barrier, inc=1, device_id=peer, device_id_type=pl.DeviceIdType.MESH)
+    pl.semaphore_wait(barrier, len(peers))
+
+
+def span(start, size):
+    return pl.ds(pl.multiple_of(start, 16), size)
+
+
+def exchange(source, target, size, mine, group, axis, sems):
+    made = []
+    for d, peer in enumerate(group):
+        copied = pltpu.make_async_remote_copy(
+            src_ref=source.at[span(peer[axis] * size, size)],
+            dst_ref=target.at[span(mine * size, size)],
+            send_sem=sems.at[0, d], recv_sem=sems.at[1, d], device_id=peer,
+            device_id_type=pl.DeviceIdType.MESH,
+        )
+        copied.start()
+        made.append(copied)
+    target[span(mine * size, size), :] = source[span(mine * size, size), :]
+    return made
+
+
+def finished(made):
+    for copied in made:
+        copied.wait()
+
+
+def front(cfg, lat_ref, cot_ref, w_row_ref, gain_row_ref, w_ref, gain_ref,
+          ur_ref, ar_ref, out_ref, dmid_ref, dw_ref,
+          x_ref, mid_ref, hop1, turned, hop2, send_ref, c_ref, n_ref, q_ref, k_ref, v_ref,
+          u_ref, g_ref, a_ref, da_ref, dq_ref, dk_ref, dv_ref, lat_sem, cot_sem, hop1_sem, hop2_sem):
     nr, nc, ri, cj = cfg
-    ct = nr * cj
-    u_ref[...] = reorder(x_ref[...], (nc, ri, ct), (1, 0, 2))
-    uf = u_ref[...].astype(F32)
+    rt, ct = nc * ri, nr * cj
+    tokens = lat_ref.shape[0]
+    r, c = lax.axis_index("row"), lax.axis_index("col")
+    row_peer = [(lax.rem(r + d, nr), c) for d in range(1, nr)]
+    col_peer = [(r, lax.rem(c + d, nc)) for d in range(1, nc)]
+    greet(row_peer + col_peer)
+    lat = exchange(lat_ref, x_ref, tokens // nc, c, col_peer, 1, lat_sem)
+    send_ref[...] = reorder(cot_ref[...], (rt, ct), (1, 0))
+    cot = exchange(send_ref, c_ref, tokens // nr, r, row_peer, 0, cot_sem)
+    finished(lat)
+    ur_ref[...] = reorder(x_ref[...], (nc, ri, ct), (1, 0, 2))
+    uf = ur_ref[...].astype(F32)
     n_ref[...] = (uf * inverse_rms(uf)).astype(BF)
     for i, ref in enumerate((q_ref, k_ref, v_ref)):
-        ref[...] = dot(n_ref[...], w_ref[i]).astype(BF)
-    attention(ri, q_ref, k_ref, v_ref, a_ref, None, None, None, None, gain_ref)
-    mid = (u_ref[...].astype(F32) + dot(a_ref[...], w_ref[3])).astype(BF)
-    mid_ref[...] = reorder(mid, (ri, nc, nr, cj), (2, 1, 3, 0))
-
-
-def column(cfg, x_ref, c_ref, w_ref, gain_ref, out_ref, dmid_ref, dw_ref,
-           u_ref, g_ref, n_ref, q_ref, k_ref, v_ref, a_ref, da_ref, dq_ref, dk_ref, dv_ref):
-    nr, nc, ri, cj = cfg
-    rt = nc * ri
+        ref[...] = dot(n_ref[...], w_row_ref[i]).astype(BF)
+    attention(ri, q_ref, k_ref, v_ref, ar_ref, None, None, None, None, gain_row_ref)
+    mid = (ur_ref[...].astype(F32) + dot(ar_ref[...], w_row_ref[3])).astype(BF)
+    mid_ref[...] = reorder(mid, (ri, nc, nr, cj), (1, 2, 3, 0))
+    made = exchange(mid_ref, hop1, tokens // nc, c, col_peer, 1, hop1_sem)
+    finished(cot)
     g_ref[...] = reorder(c_ref[...], (nr, cj, rt), (1, 0, 2))
     da_ref[...] = (dot(g_ref[...], w_ref[3], 1, 1) * gain_ref[...]).astype(BF)
-    u_ref[...] = reorder(x_ref[...], (nr * nc, cj, ri), (1, 0, 2))
+    finished(made)
+    turned[...] = reorder(hop1[...], (nc, nr, cj * ri), (1, 0, 2))
+    finished(exchange(turned, hop2, tokens // nr, r, row_peer, 0, hop2_sem))
+    u_ref[...] = reorder(hop2[...], (nr * nc, cj, ri), (1, 0, 2))
     uf = u_ref[...].astype(F32)
     n_ref[...] = (uf * inverse_rms(uf)).astype(BF)
     for i, ref in enumerate((q_ref, k_ref, v_ref)):
         ref[...] = dot(n_ref[...], w_ref[i]).astype(BF)
     attention(cj, q_ref, k_ref, v_ref, a_ref, da_ref, dq_ref, dk_ref, dv_ref, gain_ref)
     dmid = input_grad(g_ref[...], u_ref[...], dq_ref, dk_ref, dv_ref, w_ref)
-    dmid_ref[...] = reorder(dmid, (cj, nr * nc, ri), (1, 0, 2))
+    dmid_ref[...] = reorder(dmid, (cj, nr, nc, ri), (1, 2, 0, 3))
     out = (u_ref[...].astype(F32) + dot(a_ref[...], w_ref[3])).astype(BF)
     out_ref[...] = reorder(out, (cj, nr, rt), (1, 0, 2))
     weight_grads(dw_ref, n_ref, a_ref, g_ref, dq_ref, dk_ref, dv_ref)
@@ -152,13 +194,7 @@
     z_peer = [(r, lax.rem(z + d, nz) * 2 + core) for d in range(1, nz)]
     peers = row_peer + col_peer
 
-    barrier = pltpu.get_barrier_semaphore()
-    for peer in peers:
-        pl.semaphore_signal(barrier, inc=1, device_id=peer, device_id_type=pl.DeviceIdType.MESH)
-    pl.semaphore_wait(barrier, len(peers))
-
-    def span(start, size):
-        return pl.ds(pl.multiple_of(start, 16), size)
+    greet(peers)
 
     def copy(part, slot, source, target, peer):
         made = pltpu.make_async_remote_copy(
@@ -228,24 +264,6 @@
                 made.append(copy(part, slot, block, block, peer))
                 slot += 1
             yield made
-
-    def exchange(source, target, size, mine, group, axis, sems):
-        made = []
-        for d, peer in enumerate(group):
-            copied = pltpu.make_async_remote_copy(
-                src_ref=source.at[span(peer[axis] * size, size)],
-                dst_ref=target.at[span(mine * size, size)],
-                send_sem=sems.at[0, d], recv_sem=sems.at[1, d], device_id=peer,
-                device_id_type=pl.DeviceIdType.MESH,
-            )
-            copied.start()
-            made.append(copied)
-        target[span(mine * size, size), :] = source[span(mine * size, size), :]
-        return made
-
-    def finished(made):
-        for copied in made:
-            copied.wait()
 
     flying = {}
 
@@ -335,20 +353,6 @@
     return total[1].astype(F32), total[0].astype(F32), glat
 
 
-def call(kernel, name, n_in, outs, scratch, flops):
-    vmem = pl.BlockSpec(memory_space=pltpu.VMEM)
-    return pl.pallas_call(
-        kernel,
-        name=name,
-        out_shape=outs,
-        in_specs=[vmem] * n_in,
-        out_specs=[vmem] * len(outs),
-        scratch_shapes=scratch,
-        compiler_params=pltpu.CompilerParams(vmem_limit_bytes=24 * 2**20),
-        cost_estimate=pl.CostEstimate(flops=flops, bytes_accessed=6 * 2**20, transcendentals=0),
-    )
-
-
 def body(sizes, latents, cotangent, w_row, w_col, keep_heads):
     nr, nc = sizes
     rt, ct, width = latents.shape
@@ -361,22 +365,27 @@
     act = jax.ShapeDtypeStruct(flat, BF)
     dw = jax.ShapeDtypeStruct((w_row.shape[0] * width, width), BF)
     tile = pltpu.VMEM(flat, BF)
-    unit = 2 * tokens * width * width
-
-    def exchange(values, axes, parts):
-        pieces = values.reshape(parts, tokens // parts, width)
-        return lax.all_to_all(pieces, axes, split_axis=0, concat_axis=0, tiled=True).reshape(flat)
-
-    x_rows = exchange(latents, "col", nc)
-    g_cols = exchange(cotangent.transpose(1, 0, 2), "row", nr)
-    mid, *saved = call(
-        functools.partial(row_forward, cfg), "row_forward", 3, [act] * 3, [tile] * 4, 6 * unit
-    )(x_rows, w_row, gain_row)
-    x_cols = exchange(mid, ("row", "col"), nr * nc)
-    out, dmid, dw_col = call(
-        functools.partial(column, cfg), "column", 4, [act, act, dw], [tile] * 11, 16 * unit
-    )(x_cols, g_cols, w_col, gain_col)
-    output = exchange(out, "row", nr).reshape(ct, rt, width).transpose(1, 0, 2)
+    vmem = pl.BlockSpec(memory_space=pltpu.VMEM)
+    saved_u, saved_a, out, dmid, dw_col = pl.pallas_call(
+        functools.partial(front, cfg),
+        name="front",
+        out_shape=[act, act, act, act, dw],
+        in_specs=[vmem] * 6,
+        out_specs=[vmem] * 5,
+        scratch_shapes=[tile] * 18 + [
+            pltpu.SemaphoreType.DMA((2, n - 1)) for n in (nc, nr, nc, nr)
+        ],
+        compiler_params=pltpu.CompilerParams(
+            collective_id=1, has_side_effects=True, vmem_limit_bytes=36 * 2**20
+        ),
+        cost_estimate=pl.CostEstimate(
+            flops=10**10, bytes_accessed=100 * 2**20, transcendentals=0
+        ),
+    )(latents.reshape(flat), cotangent.reshape(flat), w_row, gain_row, w_col, gain_col)
+    saved = (saved_u, saved_a)
+    pieces = out.reshape(nr, tokens // nr, width)
+    output = lax.all_to_all(pieces, "row", split_axis=0, concat_axis=0, tiled=True)
+    output = output.reshape(ct, rt, width).transpose(1, 0, 2)
     grad_row, grad_col, glat = last_kernel(cfg, dmid, dw_col, w_row, gain_row, saved)
     grad_latents = glat.reshape(latents.shape)
     return (output, grad_latents, grad_row, grad_col)

time: 169 us -> 164 us (0.970)
  Pallas kernels: 99.5 us -> 138 us
  waiting for transfers between devices: 29.4 us -> 0.01 us
  starting transfers between devices: 17.8 us -> 4.33 us
    pallas_call x2 -> x1, Pallas kernels: 20.1 us -> 51.7 us  [body(): pl.pallas_call(functools.partial(front, cfg), name='front', out_shape=[ac...]
    all_to_all x4 -> x1, waiting for transfers between devices: 29.4 us -> 0.01 us  [body(): lax.all_to_all(pieces, 'row', split_axis=0, concat_axis=0, tiled=True)]
    all_to_all x4 -> x1, starting transfers between devices: 17.8 us -> 4.33 us  [body(): lax.all_to_all(pieces, 'row', split_axis=0, concat_axis=0, tiled=True)]
    pallas_call x1, Pallas kernels: 79.4 us -> 86.2 us  [last_kernel(): pl.pallas_call(functools.partial(finish, cfg, parts), name='finish', out_...]
    unnamed x27 -> x24, local copies, waits for them, and re-layouts: 14.8 us -> 14 us
  transfers between devices with their start and end apart: 4 -> 1, of which waited for: 2 -> 0; matrix products, arithmetic and copies ran while one was open for 5% -> 3% of each run, Pallas kernels for 51% -> 53%
where the time goes in v4:
time: 164 us; the launch traced here: 163 us
  Pallas kernels  138 us (84%)
  local copies, waits for them, and re-layouts  14.5 us (9%)
  other arithmetic  5.89 us (4%)
  starting transfers between devices  4.33 us (3%)
    pallas_call x1, Pallas kernels, last_kernel(): pl.pallas_call(functools.partial(finish, cfg, parts), name='finish', out_...  86.2 us
    pallas_call x1, Pallas kernels, body(): pl.pallas_call(functools.partial(front, cfg), name='front', out_shape=[ac...  51.7 us
    unnamed x24, local copies, waits for them, and re-layouts  14 us
    convert_element_type x2, other arithmetic, last_kernel(): return (total[1].astype(F32), total[0].astype(F32), glat)  5.21 us
    all_to_all x1, starting transfers between devices, body(): lax.all_to_all(pieces, 'row', split_axis=0, concat_axis=0, tiled=True)  4.33 us
  transfers between devices with their start and end apart: 1, of which 0 were waited for; matrix products, arithmetic and copies ran while one was open for 3% of the time, Pallas kernels for 53%

profile of v4, /device:TPU:0, one launch (start us, length us, event | category | flops | bytes accessed | tf_op | source)
XLA Modules:
  0.0 163.4 jit_solution(10589534802947605360)
XLA Ops:
  0.6 0.7 convert_element_type.15
  1.3 0.1 broadcast_in_dim.11
  1.4 0.1 broadcast_in_dim.12.gain_ref
  1.5 0.1 broadcast_in_dim.9
  1.5 0.1 broadcast_in_dim.10.gain_row_ref.gain_ref
  1.6 1.6 copy-done
  3.2 1.6 copy-done.8
  4.8 1.0 copy-done.9
  5.8 1.0 copy-done.10
  6.9 51.7 %front.1 = (bf16[512,512]{1,0:T(8,128)(2,1)S(1)}, bf16[512,512]{1,0:T(8,128)(2,1)S(1)}, bf16[512,512]{1,0:T(8,128)(2,1)}, bf16[512,512]{1,0:T(8,128)(2,1)S(1)}, bf16[2048,512]{1,0:T(8,128)(2,1)S(1)}) custom-call(bf16[512,512]{1,0:T(8,128)(2,1)S(1)} %bitcast.16, bf16[512,512]{1,0:T(8,128)(2,1)S(1)} %bitcast.17, bf16[4,512,512]{2,1,0:T(8,128)(2,1)S(1)} %copy-done, ...), custom_call_target="tpu_custom_call" | custom-call | flops 10000000000 | bytes 104857600 | tf_op jit(solution)/shard_map/front/pallas_call | solution.py:369
  58.6 0.0 copy-start.2
  58.6 1.3 copy-done.2
  60.0 0.8 copy-done.6
  60.8 4.3 %all-to-all-start = ((bf16[4,128,512]{2,1,0:T(8,128)(2,1)}), bf16[4,128,512]{2,1,0:T(8,128)(2,1)}, u32[]{:S(2)}, u32[]{:S(2)}) async-start(bf16[4,128,512]{2,1,0:T(8,128)(2,1)} %bitcast.4), calls=%async_computation | async-start | bytes 1048576 | tf_op jit(solution)/shard_map/all_to_all | solution.py:387
  65.1 0.0 copy-start.3
  65.1 1.6 copy-done.3
  66.7 1.0 copy-done.5
  67.7 1.0 copy-done.7
  68.8 86.2 %finish.1 = (bf16[4096,512]{1,0:T(8,128)(2,1)S(1)}, bf16[512,512]{1,0:T(8,128)(2,1)S(1)}) custom-call(bf16[512,512]{1,0:T(8,128)(2,1)S(1)} %copy-done.7, bf16[2048,512]{1,0:T(8,128)(2,1)S(1)} %copy-done.3, bf16[4,512,512]{2,1,0:T(8,128)(2,1)S(1)} %copy-done.1, f32[1,512]{1,0:T(1,128)S(1)} %broadcast_in_dim.10.gain_row_ref.gain_ref, ...), custom_call_target="tpu_custom_call" | custom-call | flops 1000000000 | bytes 209715200 | tf_op jit(solution)/shard_map/finish/pallas_call | solution.py:327
  155.0 0.3 fusion
  155.3 2.6 %convert.2 = f32[4,512,512]{2,1,0:T(8,128)} convert(bf16[4,512,512]{2,1,0:T(8,128)(2,1)S(1)} %bitcast.19) | non-fusion elementwise | flops 1048576 | bytes 6291456 | tf_op jit(solution)/shard_map/convert_element_type | solution.py:353
  157.9 2.6 %convert.3 = f32[4,512,512]{2,1,0:T(8,128)} convert(bf16[4,512,512]{2,1,0:T(8,128)(2,1)S(1)} %bitcast.18) | non-fusion elementwise | flops 1048576 | bytes 6291456 | tf_op jit(solution)/shard_map/convert_element_type | solution.py:353
  160.5 2.1 %copy.9 = bf16[32,16,512]{2,1,0:T(8,128)(2,1)} copy(bf16[32,16,512]{2,0,1:T(8,128)(2,1)} %bitcast.6) | data formatting | bytes 1048576
  162.6 0.8 copy.11
  (13 shorter events, 0.0 us)
Async XLA Ops:
  1.6 1.6 copy-start
  3.2 1.6 copy-start.8
  4.8 1.0 copy-start.9
  5.8 1.0 copy-start.10
  6.9 58.2 %copy-start.1 = (bf16[4,512,512]{2,1,0:T(8,128)(2,1)S(1)}, bf16[4,512,512]{2,1,0:T(8,128)(2,1)}, u32[]{:S(2)}) copy-start(bf16[4,512,512]{2,1,0:T(8,128)(2,1)} %w_ref.3) | copy-start | bytes 6291460
  58.6 1.3 copy-start.2
  60.0 0.8 copy-start.6
  60.7 4.3 %copy-start.4 = (bf16[512,512]{1,0:T(8,128)(2,1)}, bf16[512,512]{1,0:T(8,128)(2,1)S(1)}, u32[]{:S(2)}) copy-start(bf16[512,512]{1,0:T(8,128)(2,1)S(1)} %get-tuple-element.15.a_ref) | copy-start | bytes 1572868
  60.8 99.8 %all-to-all-start = ((bf16[4,128,512]{2,1,0:T(8,128)(2,1)}), bf16[4,128,512]{2,1,0:T(8,128)(2,1)}, u32[]{:S(2)}, u32[]{:S(2)}) async-start(bf16[4,128,512]{2,1,0:T(8,128)(2,1)} %bitcast.4), calls=%async_computation | async-start | bytes 1048576 | tf_op jit(solution)/shard_map/all_to_all | solution.py:387
  65.1 1.6 copy-start.3
  66.7 1.0 copy-start.5
  67.7 1.0 copy-start.7
